TPU v7x, 32 devices: a whole 2x2x4 slice. The times are simulated.
32 devices in a mesh: dp: 32 (over z, y, x, core).
Axes of the slice: x: 2, y: 2, z: 4, core: 2. Of those that a mesh axis runs over, the one named last changes fastest.
Arguments:
- word_states: bfloat16 [16384, 768], P('dp'), may hold values from -6 to 6
- word_segments: int32 [32, 512], P('dp'), may hold values from 0 to 3, never falling along the last dimension, each value on 1 to 384 neighbouring positions
- entity_segments: int32 [32, 128], P('dp'), may hold values from 0 to 3, never falling along the last dimension, each value on 1 to 96 neighbouring positions
- request_rows: int32 [1024, 10], P('dp'), may hold values from 0 to 3967
- request_slot: int32 [1024, 10], P('dp'), may hold values from 0 to 160, as said below
- mask_slots: int32 [32, 32], P('dp'), may hold values from 0 to 127, as said below
- entity_table: bfloat16 [126976, 256], P('dp'), may hold values from -0.75 to 0.75
- vocab_bias: bfloat16 [126976], P('dp'), may hold values from 71 to 89
- entity_dense: bfloat16 [256, 768], replicated, may hold values from -3 to 3
- query_ww: bfloat16 [768, 768], replicated, may hold values from -0.21875 to 0.21875
- query_we: bfloat16 [768, 768], replicated, may hold values from -0.21875 to 0.21875
- query_ew: bfloat16 [768, 768], replicated, may hold values from -0.21875 to 0.21875
- query_ee: bfloat16 [768, 768], replicated, may hold values from -0.21875 to 0.21875
- key_weight: bfloat16 [768, 768], replicated, may hold values from -0.21875 to 0.21875
- value_weight: bfloat16 [768, 768], replicated, may hold values from -0.21875 to 0.21875
- out_weight: bfloat16 [768, 768], replicated, may hold values from -2 to 2
- norm1_gain: float32 [768], replicated, may hold values from 0.25 to 1.75
- norm1_bias: float32 [768], replicated, may hold values from -1.8 to 1.8
- up_weight: bfloat16 [768, 3072], replicated, may hold values from -0.21875 to 0.21875
- down_weight: bfloat16 [3072, 768], replicated, may hold values from -0.21875 to 0.21875
- norm2_gain: float32 [768], replicated, may hold values from 0.25 to 1.75
- norm2_bias: float32 [768], replicated, may hold values from -1.8 to 1.8
- head_weight: bfloat16 [768, 256], replicated, may hold values from -0.21875 to 0.21875
- head_gain: float32 [256], replicated, may hold values from 0.25 to 1.75
- head_bias: float32 [256], replicated, may hold values from -1.8 to 1.8
- cotangent: bfloat16 [20480, 768], P('dp'), may hold values from -2.9206276e-05 to 2.9206276e-05
Outputs:
- loss: float32 [], replicated
- layer_out: bfloat16 [20480, 768], P('dp')
- grad_words: bfloat16 [16384, 768], P('dp')
- grad_table: float32 [126976, 256], P('dp')
- grad_vocab_bias: float32 [126976], P('dp')
- grad_entity_dense: float32 [256, 768], P('dp')
- grad_query_ww: float32 [768, 768], P('dp')
- grad_query_we: float32 [768, 768], P('dp')
- grad_query_ew: float32 [768, 768], P('dp')
- grad_query_ee: float32 [768, 768], P('dp')
- grad_key: float32 [768, 768], P('dp')
- grad_value: float32 [768, 768], P('dp')
- grad_out: float32 [768, 768], P('dp')
- grad_norm1_gain: float32 [768], P('dp')
- grad_norm1_bias: float32 [768], P('dp')
- grad_up: float32 [768, 3072], P('dp')
- grad_down: float32 [3072, 768], P('dp')
- grad_norm2_gain: float32 [768], P('dp')
- grad_norm2_bias: float32 [768], P('dp')
- grad_head_weight: float32 [768, 256], P('dp')
- grad_head_gain: float32 [256], P('dp')
- grad_head_bias: float32 [256], P('dp')
- mask_loss: float32 [1024], P('dp')
Inputs may be any that keep to these rules, and one draw needn't show every extreme that they name: `request_slot`: row block s * 32 + o holds the entries that sequence s sends to owner o: each request number below 160 appears exactly once among a sequence's entries, 160 marks an empty entry; some owner receives 10 requests from every sequence. `request_rows`: rows of empty entries are ignored. `mask_slots`: distinct within a sequence. `word_segments`: never falling along a sequence; every document 0 to 3 has words, one has exactly 384. `entity_segments`: never falling along a sequence; every document 0 to 3 has entity slots, one has exactly 96.
All inputs are finite; a program needn't handle non-finite values.
Results may differ from a plain program's by a relative error of at most 0.029.
Values may be sent and summed in bfloat16 or wider, within the bound.
A program may use at most 192 MiB of HBM per device.

v0:
```python
import jax
import jax.numpy as jnp
from jax import lax
from jax.sharding import PartitionSpec as P

HD = 64


EPSILON = 1e-05
MASKED = -1000000000.0


def dot_plain(left_side, right_side):
    return jnp.dot(left_side, right_side, preferred_element_type=jnp.float32)


def dot_left_t(left_side, right_side):
    return lax.dot_general(
        left_side, right_side, (((0,), (0,)), ((), ())), preferred_element_type=jnp.float32
    )


def dot_right_t(left_side, right_side):
    return lax.dot_general(
        left_side, right_side, (((1,), (1,)), ((), ())), preferred_element_type=jnp.float32
    )


def dot_exact(left_side, right_side):
    return jnp.dot(
        left_side, right_side, precision=lax.Precision.HIGHEST, preferred_element_type=jnp.float32
    )


def layer_norm(tensor, gain_vec, shift_vec):
    center = tensor - jnp.mean(tensor, axis=-1, keepdims=True)
    spread = jnp.mean(center * center, axis=-1, keepdims=True)
    return center * lax.rsqrt(spread + EPSILON) * gain_vec + shift_vec


def gelu_exact(tensor):
    return jax.nn.gelu(tensor, approximate=False)


def head_act(tensor, gain_vec, shift_vec):
    return layer_norm(gelu_exact(tensor), gain_vec, shift_vec)


def norm_back(tensor, gain_vec, shift_vec, grad_out):
    result, pullback = jax.vjp(layer_norm, tensor, gain_vec, shift_vec)
    return pullback(grad_out)


def attn_scores(query_word, query_entity, key_rows, allowed, word_count):
    to_words = jnp.einsum(
        "qhd,khd->hqk", query_word, key_rows[:word_count], preferred_element_type=jnp.float32
    )
    to_entities = jnp.einsum(
        "qhd,khd->hqk", query_entity, key_rows[word_count:], preferred_element_type=jnp.float32
    )
    return jnp.where(allowed[None], jnp.concatenate([to_words, to_entities], axis=2), MASKED)


def body(
    word_states,
    word_segments,
    entity_segments,
    request_rows,
    request_slot,
    mask_slots,
    entity_table,
    vocab_bias,
    entity_dense,
    query_ww,
    query_we,
    query_ew,
    query_ee,
    key_weight,
    value_weight,
    out_weight,
    norm1_gain,
    norm1_bias,
    up_weight,
    down_weight,
    norm2_gain,
    norm2_bias,
    head_weight,
    head_gain,
    head_bias,
    cotangent,
):
    word_count = word_states.shape[0]
    model_width = word_states.shape[1]
    slot_count = entity_segments.shape[1]
    mask_count = mask_slots.shape[1]
    request_count = slot_count + mask_count
    seq_len = word_count + slot_count
    devices = lax.axis_size("dp")
    capacity = request_rows.shape[1]
    head_count = model_width // HD
    query_scale = HD ** (-0.5)
    emb_width = entity_table.shape[1]
    table_rows = entity_table.shape[0]
    total_mask = mask_count * devices
    grad_scale = 1.0 / total_mask
    asked_ids = lax.all_to_all(request_rows, "dp", split_axis=0, concat_axis=0, tiled=True)
    found_rows = jnp.take(entity_table, asked_ids, axis=0)
    found_bias = jnp.take(vocab_bias, asked_ids, axis=0)
    back_rows = lax.all_to_all(found_rows, "dp", split_axis=0, concat_axis=0, tiled=True)
    back_bias = lax.all_to_all(found_bias, "dp", split_axis=0, concat_axis=0, tiled=True)
    got_rows = back_rows
    got_bias = back_bias
    slot_ids = request_slot.reshape(devices * capacity)
    placing = slot_ids[None, :] == jnp.arange(request_count, dtype=jnp.int32)[:, None]
    placing_low = placing.astype(jnp.bfloat16)
    request_vecs = dot_plain(placing_low, got_rows.reshape(devices * capacity, emb_width))
    request_bias = dot_plain(placing_low, got_bias.reshape(devices * capacity, 1))[:, 0]
    entity_low = request_vecs[:slot_count].astype(jnp.bfloat16)
    target_vecs = request_vecs[slot_count:]
    target_bias = request_bias[slot_count:]
    entity_states = dot_plain(entity_low, entity_dense)
    hidden = jnp.concatenate([word_states.astype(jnp.float32), entity_states], axis=0)
    hidden_low = hidden.astype(jnp.bfloat16)
    word_part = hidden_low[:word_count]
    entity_part = hidden_low[word_count:]
    query_word = (
        query_scale
        * jnp.concatenate(
            [dot_plain(word_part, query_ww), dot_plain(entity_part, query_ew)], axis=0
        )
    ).astype(jnp.bfloat16)
    query_entity = (
        query_scale
        * jnp.concatenate(
            [dot_plain(word_part, query_we), dot_plain(entity_part, query_ee)], axis=0
        )
    ).astype(jnp.bfloat16)
    key_rows = dot_plain(hidden_low, key_weight).astype(jnp.bfloat16)
    values = dot_plain(hidden_low, value_weight).astype(jnp.bfloat16)
    head_shape = (seq_len, head_count, HD)
    query_word_h = query_word.reshape(head_shape)
    query_entity_h = query_entity.reshape(head_shape)
    key_rows_h = key_rows.reshape(head_shape)
    values_h = values.reshape(head_shape)
    segment_row = jnp.concatenate([word_segments[0], entity_segments[0]])
    allowed = segment_row[:, None] == segment_row[None, :]
    scores = attn_scores(query_word_h, query_entity_h, key_rows_h, allowed, word_count)
    row_top = jnp.max(scores, axis=2, keepdims=True)
    exp_scores = jnp.exp(scores - row_top)
    row_total = jnp.sum(exp_scores, axis=2, keepdims=True)
    attn_low = (exp_scores / row_total).astype(jnp.bfloat16)
    row_lse = row_top + jnp.log(row_total)
    context = jnp.einsum("hqk,khd->qhd", attn_low, values_h, preferred_element_type=jnp.float32)
    context_low = context.reshape(seq_len, model_width).astype(jnp.bfloat16)
    attended = dot_plain(context_low, out_weight)
    residual_one = hidden + attended
    normed = layer_norm(residual_one, norm1_gain, norm1_bias)
    normed_low = normed.astype(jnp.bfloat16)
    up_value = dot_plain(normed_low, up_weight)
    activated = gelu_exact(up_value).astype(jnp.bfloat16)
    down_value = dot_plain(activated, down_weight)
    residual_two = normed + down_value
    layer_out = layer_norm(residual_two, norm2_gain, norm2_bias)
    choose = (mask_slots[0][:, None] == jnp.arange(slot_count, dtype=jnp.int32)[None, :]).astype(
        jnp.float32
    )
    picked_low = dot_exact(choose, layer_out[word_count:]).astype(jnp.bfloat16)
    head_pre = dot_plain(picked_low, head_weight)
    head_low = head_act(head_pre, head_gain, head_bias).astype(jnp.bfloat16)
    head_f32 = head_low.astype(jnp.float32)
    target_logit = jnp.sum(head_f32 * target_vecs, axis=1) + target_bias
    all_heads = lax.all_gather(head_low, "dp", axis=0, tiled=True)
    block_rows = min(512, total_mask)
    block_count = total_mask // block_rows
    bias_f32 = vocab_bias.astype(jnp.float32)

    def block_logits(block_index):
        row_block = lax.dynamic_slice_in_dim(all_heads, block_index * block_rows, block_rows, 0)
        return (row_block, dot_right_t(row_block, entity_table) + bias_f32[None, :])

    def block_stats(block_index):
        row_block, logits = block_logits(block_index)
        top_value = jnp.max(logits, axis=1)
        return (top_value, jnp.sum(jnp.exp(logits - top_value[:, None]), axis=1))

    local_top, local_total = lax.map(block_stats, jnp.arange(block_count, dtype=jnp.int32))
    local_top = local_top.reshape(total_mask)
    local_total = local_total.reshape(total_mask)
    target_sum = jnp.sum(target_logit)
    global_top = lax.pmax(local_top, "dp")
    global_total, target_total = lax.psum(
        (local_total * jnp.exp(local_top - global_top), target_sum), "dp"
    )
    lse_all = global_top + jnp.log(global_total)
    loss_value = (jnp.sum(lse_all) - target_total) * grad_scale
    own_lse = lax.dynamic_slice_in_dim(lse_all, lax.axis_index("dp") * mask_count, mask_count, 0)
    mask_loss = own_lse - target_logit

    def block_back(running, block_index):
        table_grad, bias_grad = running
        row_block, logits = block_logits(block_index)
        lse_block = lax.dynamic_slice_in_dim(lse_all, block_index * block_rows, block_rows, 0)
        logit_grad = (jnp.exp(logits - lse_block[:, None]) * grad_scale).astype(jnp.bfloat16)
        table_grad = table_grad + dot_left_t(logit_grad, row_block)
        bias_grad = bias_grad + jnp.sum(logit_grad.astype(jnp.float32), axis=0)
        return ((table_grad, bias_grad), dot_plain(logit_grad, entity_table))

    start_grads = (
        jnp.zeros((table_rows, emb_width), jnp.float32),
        jnp.zeros((table_rows,), jnp.float32),
    )
    (table_grad, bias_grad), head_terms = lax.scan(
        block_back, start_grads, jnp.arange(block_count, dtype=jnp.int32)
    )
    head_grad = lax.psum_scatter(
        head_terms.reshape(total_mask, emb_width), "dp", scatter_dimension=0, tiled=True
    )
    head_grad = head_grad - grad_scale * target_vecs
    target_grad = -grad_scale * head_f32
    pre_grad, head_gain_grad, head_bias_grad = jax.vjp(head_act, head_pre, head_gain, head_bias)[1](
        head_grad
    )
    pre_low = pre_grad.astype(jnp.bfloat16)
    head_weight_grad = dot_left_t(picked_low, pre_low)
    picked_grad = dot_right_t(pre_low, head_weight)
    out_grad = cotangent.astype(jnp.float32) + jnp.concatenate(
        [jnp.zeros((word_count, model_width), jnp.float32), dot_exact(choose.T, picked_grad)],
        axis=0,
    )
    resid_grad, norm2_gain_grad, norm2_bias_grad = norm_back(
        residual_two, norm2_gain, norm2_bias, out_grad
    )
    down_in = resid_grad.astype(jnp.bfloat16)
    down_grad = dot_left_t(activated, down_in)
    act_grad = dot_right_t(down_in, down_weight)
    up_grad = jax.vjp(gelu_exact, up_value)[1](act_grad)[0]
    up_low = up_grad.astype(jnp.bfloat16)
    up_weight_grad = dot_left_t(normed_low, up_low)
    normed_grad = resid_grad + dot_right_t(up_low, up_weight)
    first_grad, norm1_gain_grad, norm1_bias_grad = norm_back(
        residual_one, norm1_gain, norm1_bias, normed_grad
    )
    attn_in = first_grad.astype(jnp.bfloat16)
    out_weight_grad = dot_left_t(context_low, attn_in)
    context_grad = dot_right_t(attn_in, out_weight).astype(jnp.bfloat16).reshape(head_shape)
    scores_again = attn_scores(query_word_h, query_entity_h, key_rows_h, allowed, word_count)
    attn_prob = jnp.exp(scores_again - row_lse)
    prob_low = attn_prob.astype(jnp.bfloat16)
    prob_grad = jnp.einsum(
        "qhd,khd->hqk", context_grad, values_h, preferred_element_type=jnp.float32
    )
    values_grad = jnp.einsum(
        "hqk,qhd->khd", prob_low, context_grad, preferred_element_type=jnp.float32
    )
    values_grad = values_grad.reshape(seq_len, model_width).astype(jnp.bfloat16)
    row_delta = jnp.sum(attn_prob * prob_grad, axis=2, keepdims=True)
    score_grad = (attn_prob * (prob_grad - row_delta)).astype(jnp.bfloat16)
    qword_grad = jnp.einsum(
        "hqk,khd->qhd",
        score_grad[:, :, :word_count],
        key_rows_h[:word_count],
        preferred_element_type=jnp.float32,
    )
    qword_grad = qword_grad.reshape(seq_len, model_width).astype(jnp.bfloat16)
    qent_grad = jnp.einsum(
        "hqk,khd->qhd",
        score_grad[:, :, word_count:],
        key_rows_h[word_count:],
        preferred_element_type=jnp.float32,
    )
    qent_grad = qent_grad.reshape(seq_len, model_width).astype(jnp.bfloat16)
    keys_grad = jnp.concatenate(
        [
            jnp.einsum(
                "hqk,qhd->khd",
                score_grad[:, :, :word_count],
                query_word_h,
                preferred_element_type=jnp.float32,
            ),
            jnp.einsum(
                "hqk,qhd->khd",
                score_grad[:, :, word_count:],
                query_entity_h,
                preferred_element_type=jnp.float32,
            ),
        ],
        axis=0,
    )
    keys_grad = keys_grad.reshape(seq_len, model_width).astype(jnp.bfloat16)
    query_ww_grad = query_scale * dot_left_t(word_part, qword_grad[:word_count])
    query_ew_grad = query_scale * dot_left_t(entity_part, qword_grad[word_count:])
    query_we_grad = query_scale * dot_left_t(word_part, qent_grad[:word_count])
    query_ee_grad = query_scale * dot_left_t(entity_part, qent_grad[word_count:])
    key_weight_grad = dot_left_t(hidden_low, keys_grad)
    value_weight_grad = dot_left_t(hidden_low, values_grad)
    word_back = query_scale * (
        dot_right_t(qword_grad[:word_count], query_ww)
        + dot_right_t(qent_grad[:word_count], query_we)
    )
    entity_back = query_scale * (
        dot_right_t(qword_grad[word_count:], query_ew)
        + dot_right_t(qent_grad[word_count:], query_ee)
    )
    hidden_grad = (
        first_grad
        + jnp.concatenate([word_back, entity_back], axis=0)
        + dot_right_t(keys_grad, key_weight)
        + dot_right_t(values_grad, value_weight)
    )
    words_grad = hidden_grad[:word_count].astype(jnp.bfloat16)
    state_low = hidden_grad[word_count:].astype(jnp.bfloat16)
    dense_grad = dot_left_t(entity_low, state_low)
    entity_vec_grad = dot_right_t(state_low, entity_dense)
    vec_grad = jnp.concatenate([entity_vec_grad, target_grad], axis=0)
    bias_vec_grad = jnp.concatenate(
        [jnp.zeros((slot_count,), jnp.float32), jnp.full((mask_count,), -grad_scale, jnp.float32)]
    )
    placing_f32 = placing.astype(jnp.float32)
    per_request = dot_exact(placing_f32.T, vec_grad)
    bias_request = dot_exact(placing_f32.T, bias_vec_grad[:, None])[:, 0]
    back_rows, back_bias = (
        lax.all_to_all(
            per_request.reshape(devices, capacity, emb_width).astype(jnp.bfloat16),
            "dp",
            split_axis=0,
            concat_axis=0,
            tiled=True,
        ).astype(jnp.float32),
        lax.all_to_all(
            bias_request.reshape(devices, capacity).astype(jnp.bfloat16),
            "dp",
            split_axis=0,
            concat_axis=0,
            tiled=True,
        ).astype(jnp.float32),
    )
    flat_ids = asked_ids.reshape(devices * capacity)
    table_grad = table_grad + jax.ops.segment_sum(
        back_rows.reshape(devices * capacity, emb_width), flat_ids, num_segments=table_rows
    )
    bias_grad = bias_grad + jax.ops.segment_sum(
        back_bias.reshape(devices * capacity), flat_ids, num_segments=table_rows
    )
    all_sums = tuple(
        (
            lax.psum_scatter(head_weight_grad, "dp", scatter_dimension=0, tiled=True),
            lax.psum_scatter(head_gain_grad, "dp", scatter_dimension=0, tiled=True),
            lax.psum_scatter(head_bias_grad, "dp", scatter_dimension=0, tiled=True),
            lax.psum_scatter(norm2_gain_grad, "dp", scatter_dimension=0, tiled=True),
            lax.psum_scatter(norm2_bias_grad, "dp", scatter_dimension=0, tiled=True),
            lax.psum_scatter(up_weight_grad, "dp", scatter_dimension=0, tiled=True),
            lax.psum_scatter(down_grad, "dp", scatter_dimension=0, tiled=True),
            lax.psum_scatter(norm1_gain_grad, "dp", scatter_dimension=0, tiled=True),
            lax.psum_scatter(norm1_bias_grad, "dp", scatter_dimension=0, tiled=True),
            lax.psum_scatter(out_weight_grad, "dp", scatter_dimension=0, tiled=True),
            lax.psum_scatter(query_ww_grad, "dp", scatter_dimension=0, tiled=True),
            lax.psum_scatter(query_we_grad, "dp", scatter_dimension=0, tiled=True),
            lax.psum_scatter(query_ew_grad, "dp", scatter_dimension=0, tiled=True),
            lax.psum_scatter(query_ee_grad, "dp", scatter_dimension=0, tiled=True),
            lax.psum_scatter(key_weight_grad, "dp", scatter_dimension=0, tiled=True),
            lax.psum_scatter(value_weight_grad, "dp", scatter_dimension=0, tiled=True),
            lax.psum_scatter(dense_grad, "dp", scatter_dimension=0, tiled=True),
        )
    )
    return (
        loss_value,
        layer_out.astype(jnp.bfloat16),
        words_grad,
        table_grad,
        bias_grad,
        all_sums[16],
        all_sums[10],
        all_sums[11],
        all_sums[12],
        all_sums[13],
        all_sums[14],
        all_sums[15],
        all_sums[9],
        all_sums[7],
        all_sums[8],
        all_sums[5],
        all_sums[6],
        all_sums[3],
        all_sums[4],
        all_sums[0],
        all_sums[1],
        all_sums[2],
        mask_loss,
    )


def solution(mesh):
    in_specs = (
        P("dp", None),
        P("dp", None),
        P("dp", None),
        P("dp", None),
        P("dp", None),
        P("dp", None),
        P("dp", None),
        P("dp"),
        P(),
        P(),
        P(),
        P(),
        P(),
        P(),
        P(),
        P(),
        P(),
        P(),
        P(),
        P(),
        P(),
        P(),
        P(),
        P(),
        P(),
        P("dp", None),
    )
    out_specs = (
        P(),
        P("dp", None),
        P("dp", None),
        P("dp", None),
        P("dp"),
        P("dp", None),
        P("dp", None),
        P("dp", None),
        P("dp", None),
        P("dp", None),
        P("dp", None),
        P("dp", None),
        P("dp", None),
        P("dp"),
        P("dp"),
        P("dp", None),
        P("dp", None),
        P("dp"),
        P("dp"),
        P("dp", None),
        P("dp"),
        P("dp"),
        P("dp"),
    )
    return jax.shard_map(body, mesh=mesh, in_specs=in_specs, out_specs=out_specs, check_vma=False)
```

profile of v0, /device:TPU:0, one launch (start us, length us, event | category | flops | bytes accessed | tf_op | source)
XLA Modules:
  0.0 1708.4 jit_solution(7508022189889455107)
XLA Ops:
  8.7 7.3 all-to-all-start
  27.9 3.4 all-to-all-start.1
  32.4 9.5 all-to-all-done.1
  56.2 3.5 convolution_convert_fusion.2
  71.1 3.9 copy-done.6
  75.0 3.4 fusion.10
  78.5 9.7 fusion.46
  91.2 23.9 %multiply_convert_fusion.2 = (bf16[640,3072]{1,0:T(8,128)(2,1)S(1)}, f32[640,3072]{1,0:T(8,128)}, f32[640,3072]{1,0:T(8,128)}) fusion(bf16[768,3072]{1,0:T(8,128)(2,1)} %param.48, f32[640,768]{1,0:T(8,128)S(1)} %get-tuple-element.218, f32[768]{0:T(1024)S(1)} %copy-done.72, f32[768]{0:T(1024)S(1)} %copy-done.65, f32[640]{0:T(1024)S(1)} %fusion.121, ...), kind=kOutput, calls=%fused_computation.36 | convolution fusion | flops 3150151680 | bytes 26356736 | tf_op jit(solution)/shard_map/dot_general | solution.py:14
  115.2 3.4 fusion.151
  122.5 42.4 %all_gather.3 = bf16[1024,256]{1,0:T(8,128)(2,1)} all-gather(bf16[32,256]{1,0:T(8,128)(2,1)S(1)} %get-tuple-element.195), channel_id=1, replica_groups=mesh['dp'=32] {'dp'}, dimensions={0}, use_global_device_ids=true | all-gather | bytes 540672 | tf_op jit(solution)/shard_map/all_gather | solution.py:172
  164.9 10.7 while.27
  175.7 36.9 %pmax.7 = f32[1024]{0:T(1024)S(1)} all-reduce(f32[1024]{0:T(1024)S(1)} %bitcast.180), channel_id=1, replica_groups=mesh['dp'=32] {'dp'}, use_global_device_ids=true, to_apply=%region_12.13 | all-reduce | flops 1024 | bytes 8192 | tf_op jit(solution)/shard_map/pmax | solution.py:190
  212.6 41.2 %psum.14 = f32[1024]{0:T(1024)S(1)} all-reduce(f32[1024]{0:T(1024)S(1)} %exponential_multiply_fusion), channel_id=1, replica_groups=mesh['dp'=32] {'dp'}, use_global_device_ids=true, to_apply=%region_13.14 | all-reduce | flops 1024 | bytes 8192 | tf_op jit(solution)/shard_map/psum | solution.py:191
  254.4 23.7 %while.28 = (s32[]{:T(128)}, f32[3968,256]{1,0:T(8,128)}, f32[3968]{0:T(1024)S(1)}, f32[2,512,256]{2,1,0:T(8,128)}, s32[2]{0:T(128)S(1)}, /*index=5*/bf16[1024,2...) while((s32[]{:T(128)}, f32[3968,256]{1,0:T(8,128)}, ...), condition=%wide.region_20.21_spmd.clone, body=%wide.region_18.20_spmd.clone.sunk | while | flops 3134787584 | bytes 68505448 | solution.py:212
  255.7 3.2 convert_reduce_fusion.3
  261.2 3.0 convolution_add_fusion.3
  267.6 3.2 convert_reduce_fusion.3
  273.0 3.0 convolution_add_fusion.3
  278.2 135.0 %reduce-scatter.13.cloned.1.call-done = f32[32,256]{1,0:T(8,128)} async-done(((f32[1024,256]{1,0:T(8,128)}), f32[32,256]{1,0:T(8,128)}) %reduce-scatter.13.cloned.1.call-update) | async-done | bytes 32784 | tf_op jit(solution)/shard_map/reduce_scatter | solution.py:215
  422.6 11.1 add_convert_fusion
  433.8 4.3 multiply_reduce_fusion.2
  444.4 10.2 fusion.47
  454.6 24.3 %multiply_convert_fusion.1 = bf16[12,640,640]{1,2,0:T(8,128)(2,1)} fusion(f32[12,640]{1,0:T(8,128)} %copy-done.76, bf16[640,12,64]{0,2,1:T(8,128)(2,1)} %bitcast.172, bf16[640,12,64]{0,2,1:T(8,128)(2,1)} %bitcast.168, f32[12,640,128]{1,2,0:T(8,128)} %copy-done.8, f32[12,640,512]{1,2,0:T(8,128)} %copy-done.6, pred[640,640]{0,1:T(8,128)(4,1)} %broadcast_compare_fusion), kind=kOutput, calls=%fused_computation.21 | convolution fusion | flops 1307451520 | bytes 31897600 | tf_op jit(solution)/shard_map/sub | solution.py:257
  479.0 3.7 fusion.72
  482.7 6.8 fusion.65
  506.5 4.4 fusion.136
  511.0 3.7 convolution_multiply_fusion.2
  514.8 3.6 convolution_multiply_fusion.3
  518.5 4.1 fusion.157
  522.8 4.0 fusion.156
  526.9 2.9 convolution_multiply_fusion
  532.9 8.7 fusion.137
  543.2 8.7 fusion.134
  559.8 3.8 all-to-all-done.4
  567.6 5.6 all-to-all-done.2
  577.7 3.3 scatter_fusion.1
  582.9 41.2 %all-reduce.7 = (f32[]{:T(128)}, f32[768]{0:T(1024)S(1)}, f32[768]{0:T(1024)S(1)}, f32[768]{0:T(1024)S(1)}, f32[768]{0:T(1024)S(1)}, /*index=5*/f32[256]{0:T(256)S(1)}, f32[256]{0:T(256)S(1)}) all-reduce(f32[]{:T(128)} %get-tuple-element.216, f32[768]{0:T(1024)S(1)} %copy-done.90, ...), channel_id=1, replica_groups=mesh['dp'=32] {'dp'}, use_global_device_ids=true, to_apply=%region_17.18 | all-reduce | flops 3585 | bytes 28680 | tf_op jit(solution)/shard_map/psum | solution.py:191
  629.9 6.2 scatter_fusion
  636.1 50.7 %reduce-scatter.15.cloned.1.call-done = f32[8,768]{1,0:T(8,128)} async-done(((f32[256,768]{1,0:T(8,128)}), f32[8,768]{1,0:T(8,128)}) %reduce-scatter.15.cloned.1.call-update) | async-done | bytes 24592 | tf_op jit(solution)/shard_map/reduce_scatter | solution.py:362
  686.9 104.6 %reduce-scatter.29.cloned.1.call-done = f32[24,768]{1,0:T(8,128)} async-done(((f32[768,768]{1,0:T(8,128)}), f32[24,768]{1,0:T(8,128)}) %reduce-scatter.29.cloned.1.call-update) | async-done | bytes 73744 | tf_op jit(solution)/shard_map/reduce_scatter | solution.py:355
  791.5 103.8 %reduce-scatter.19.cloned.1.call-done = f32[24,768]{1,0:T(8,128)} async-done(((f32[768,768]{1,0:T(8,128)}), f32[24,768]{1,0:T(8,128)}) %reduce-scatter.19.cloned.1.call-update) | async-done | bytes 73744 | tf_op jit(solution)/shard_map/reduce_scatter | solution.py:357
  895.2 104.6 %reduce-scatter.17.cloned.1.call-done = f32[24,768]{1,0:T(8,128)} async-done(((f32[768,768]{1,0:T(8,128)}), f32[24,768]{1,0:T(8,128)}) %reduce-scatter.17.cloned.1.call-update) | async-done | bytes 73744 | tf_op jit(solution)/shard_map/reduce_scatter | solution.py:356
  999.8 103.9 %reduce-scatter.27.cloned.1.call-done = f32[24,768]{1,0:T(8,128)} async-done(((f32[768,768]{1,0:T(8,128)}), f32[24,768]{1,0:T(8,128)}) %reduce-scatter.27.cloned.1.call-update) | async-done | bytes 73744 | tf_op jit(solution)/shard_map/reduce_scatter | solution.py:361
  1103.7 104.8 %reduce-scatter.25.cloned.1.call-done = f32[24,768]{1,0:T(8,128)} async-done(((f32[768,768]{1,0:T(8,128)}), f32[24,768]{1,0:T(8,128)}) %reduce-scatter.25.cloned.1.call-update) | async-done | bytes 73744 | tf_op jit(solution)/shard_map/reduce_scatter | solution.py:360
  1208.5 104.0 %reduce-scatter.23.cloned.1.call-done = f32[24,768]{1,0:T(8,128)} async-done(((f32[768,768]{1,0:T(8,128)}), f32[24,768]{1,0:T(8,128)}) %reduce-scatter.23.cloned.1.call-update) | async-done | bytes 73744 | tf_op jit(solution)/shard_map/reduce_scatter | solution.py:359
  1312.5 104.6 %reduce-scatter.21.cloned.1.call-done = f32[24,768]{1,0:T(8,128)} async-done(((f32[768,768]{1,0:T(8,128)}), f32[24,768]{1,0:T(8,128)}) %reduce-scatter.21.cloned.1.call-update) | async-done | bytes 73744 | tf_op jit(solution)/shard_map/reduce_scatter | solution.py:358
  1417.1 140.8 %reduce-scatter.31.cloned.1.call-done = f32[24,3072]{1,0:T(8,128)} async-done(((f32[768,3072]{1,0:T(8,128)}), f32[24,3072]{1,0:T(8,128)}) %reduce-scatter.31.cloned.1.call-update) | async-done | bytes 294928 | tf_op jit(solution)/shard_map/reduce_scatter | solution.py:351
  1557.9 142.0 %reduce-scatter.33.cloned.1.call-done = f32[96,768]{1,0:T(8,128)} async-done(((f32[3072,768]{1,0:T(8,128)}), f32[96,768]{1,0:T(8,128)}) %reduce-scatter.33.cloned.1.call-update) | async-done | bytes 294928 | tf_op jit(solution)/shard_map/reduce_scatter | solution.py:352
  (397 shorter events, 126.3 us)
Async XLA Ops:
  7.2 81.0 %copy-start = (bf16[768,768]{1,0:T(8,128)(2,1)S(1)}, bf16[768,768]{1,0:T(8,128)(2,1)}, u32[]{:S(2)}) copy-start(bf16[768,768]{1,0:T(8,128)(2,1)} %param.45) | copy-start | bytes 3538948
  7.2 16.1 copy-start.7
  8.7 14.4 all-to-all-start
  17.6 25.0 %copy-start.80 = (s32[320]{0:T(512)}, s32[320]{0:T(512)S(1)}, u32[]{:S(2)}) copy-start(s32[320]{0:T(512)S(1)} %eq.59) | copy-start | bytes 3844
  20.7 10.7 copy-start.100
  23.1 19.5 %copy-start.53 = (s32[32,1,10]{2,1,0:T(1,128)}, s32[32,1,10]{2,1,0:T(1,128)S(1)}, u32[]{:S(2)}) copy-start(s32[32,1,10]{2,1,0:T(1,128)S(1)} %all-to-all-done) | copy-start | bytes 3844
  27.9 14.0 all-to-all-start.1
  31.3 381.9 %reduce-scatter.13.cloned.1.call-start = ((), (), s32[]{:S(2)}) async-start(), calls=%async_computation.17 | async-start | bytes 1081344 | tf_op jit(solution)/shard_map/reduce_scatter | solution.py:215
  66.7 11.8 copy-start.8
  88.3 26.8 %slice-start = ((s8[4718592]{0:T(1024)(128)(4,1)}), s8[4194304]{0:T(1024)(128)(4,1)S(1)}, s32[]{:S(2)}) async-start(s8[4718592]{0:T(1024)(128)(4,1)} %bitcast.190), calls=%async_computation.29 | async-start | bytes 8388608
  90.7 24.4 %copy-start.12 = (f32[640,768]{1,0:T(8,128)}, f32[640,768]{1,0:T(8,128)S(1)}, u32[]{:S(2)}) copy-start(f32[640,768]{1,0:T(8,128)S(1)} %get-tuple-element.218) | copy-start | bytes 5898244
  90.8 347.4 %copy-start.61 = (f32[640]{0:T(1024)}, f32[640]{0:T(1024)S(1)}, u32[]{:S(2)}) copy-start(f32[640]{0:T(1024)S(1)} %broadcast_multiply_fusion.1) | copy-start | bytes 7684
  91.1 24.0 %copy-start.78 = (f32[640]{0:T(1024)}, f32[640]{0:T(1024)S(1)}, u32[]{:S(2)}) copy-start(f32[640]{0:T(1024)S(1)} %multiply_reduce_fusion.6) | copy-start | bytes 7684
  91.2 347.0 %copy-start.63 = (f32[640]{0:T(1024)}, f32[640]{0:T(1024)S(1)}, u32[]{:S(2)}) copy-start(f32[640]{0:T(1024)S(1)} %fusion.121) | copy-start | bytes 7684
  91.2 23.9 %slice-start.1 = ((s8[4718592]{0:T(1024)(128)(4,1)}), s8[524288]{0:T(1024)(128)(4,1)S(1)}, s32[]{:S(2)}) async-start(s8[4718592]{0:T(1024)(128)(4,1)} %bitcast.190), calls=%async_computation.30 | async-start | bytes 1048576
  121.8 43.1 %copy-start.98 = (f32[32]{0:T(128)}, f32[32]{0:T(128)S(1)}, u32[]{:S(2)}) copy-start(f32[32]{0:T(128)S(1)} %multiply_reduce_fusion.9) | copy-start | bytes 388
  164.9 89.5 %copy-start.2 = (f32[3968]{0:T(1024)S(1)}, f32[3968]{0:T(1024)}, u32[]{:S(2)}) copy-start(f32[3968]{0:T(1024)} %custom-call.1) | copy-start | bytes 47620
  254.4 23.8 %copy-start.58 = (f32[12,640]{1,0:T(8,128)S(1)}, f32[12,640]{1,0:T(8,128)}, u32[]{:S(2)}) copy-start(f32[12,640]{1,0:T(8,128)} %copy-done.57) | copy-start | bytes 92164
  254.4 23.8 %copy-start.69 = (f32[12,640]{1,0:T(8,128)S(1)}, f32[12,640]{1,0:T(8,128)}, u32[]{:S(2)}) copy-start(f32[12,640]{1,0:T(8,128)} %copy-done.68) | copy-start | bytes 92164
  254.4 160.2 %copy-start.99 = (f32[32]{0:T(128)S(1)}, f32[32]{0:T(128)}, u32[]{:S(2)}) copy-start(f32[32]{0:T(128)} %copy-done.98) | copy-start | bytes 388
  278.1 143.6 %copy-start.75 = (f32[1024]{0:T(1024)}, f32[1024]{0:T(1024)S(1)}, u32[]{:S(2)}) copy-start(f32[1024]{0:T(1024)S(1)} %get-tuple-element.446) | copy-start | bytes 12292
  278.1 141.0 %copy-start.10 = (f32[640,768]{1,0:T(8,128)S(1)}, f32[640,768]{1,0:T(8,128)}, u32[]{:S(2)}) copy-start(f32[640,768]{1,0:T(8,128)} %copy-done.9) | copy-start | bytes 5898244
  278.1 358.0 %reduce-scatter.35.cloned.1.call-start = ((), (), s32[]{:S(2)}) async-start(), calls=%async_computation.28 | async-start | bytes 811008 | tf_op jit(solution)/shard_map/reduce_scatter | solution.py:346
  278.2 166.3 %copy-start.76 = (f32[12,640]{1,0:T(8,128)}, f32[12,640]{1,0:T(8,128)S(1)}, u32[]{:S(2)}) copy-start(f32[12,640]{1,0:T(8,128)S(1)} %log_add_fusion) | copy-start | bytes 92164
  421.7 12.0 slice-start.2
  422.5 11.2 copy-start.30
  422.5 11.2 copy-start.92
  422.5 11.2 copy-start.13
  422.5 11.2 slice-start.3
  454.6 24.3 %copy-start.37 = (f32[128,768]{0,1:T(8,128)S(1)}, f32[128,768]{0,1:T(8,128)}, u32[]{:S(2)}) copy-start(f32[128,768]{0,1:T(8,128)} %fusion.95) | copy-start | bytes 1179652
  493.5 193.4 %reduce-scatter.15.cloned.1.call-start = ((), (), s32[]{:S(2)}) async-start(), calls=%async_computation.18 | async-start | bytes 811008 | tf_op jit(solution)/shard_map/reduce_scatter | solution.py:362
  506.4 285.1 %reduce-scatter.29.cloned.1.call-start = ((), (), s32[]{:S(2)}) async-start(), calls=%async_computation.25 | async-start | bytes 2433024 | tf_op jit(solution)/shard_map/reduce_scatter | solution.py:355
  510.9 384.3 %reduce-scatter.19.cloned.1.call-start = ((), (), s32[]{:S(2)}) async-start(), calls=%async_computation.20 | async-start | bytes 2433024 | tf_op jit(solution)/shard_map/reduce_scatter | solution.py:357
  514.7 485.1 %reduce-scatter.17.cloned.1.call-start = ((), (), s32[]{:S(2)}) async-start(), calls=%async_computation.19 | async-start | bytes 2433024 | tf_op jit(solution)/shard_map/reduce_scatter | solution.py:356
  518.4 585.3 %reduce-scatter.27.cloned.1.call-start = ((), (), s32[]{:S(2)}) async-start(), calls=%async_computation.24 | async-start | bytes 2433024 | tf_op jit(solution)/shard_map/reduce_scatter | solution.py:361
  522.5 686.0 %reduce-scatter.25.cloned.1.call-start = ((), (), s32[]{:S(2)}) async-start(), calls=%async_computation.23 | async-start | bytes 2433024 | tf_op jit(solution)/shard_map/reduce_scatter | solution.py:360
  526.9 785.6 %reduce-scatter.23.cloned.1.call-start = ((), (), s32[]{:S(2)}) async-start(), calls=%async_computation.22 | async-start | bytes 2433024 | tf_op jit(solution)/shard_map/reduce_scatter | solution.py:359
  529.9 887.2 %reduce-scatter.21.cloned.1.call-start = ((), (), s32[]{:S(2)}) async-start(), calls=%async_computation.21 | async-start | bytes 2433024 | tf_op jit(solution)/shard_map/reduce_scatter | solution.py:358
  532.8 1025.1 %reduce-scatter.31.cloned.1.call-start = ((), (), s32[]{:S(2)}) async-start(), calls=%async_computation.26 | async-start | bytes 9732096 | tf_op jit(solution)/shard_map/reduce_scatter | solution.py:351
  541.6 1158.3 %reduce-scatter.33.cloned.1.call-start = ((), (), s32[]{:S(2)}) async-start(), calls=%async_computation.27 | async-start | bytes 9732096 | tf_op jit(solution)/shard_map/reduce_scatter | solution.py:352
  553.9 9.6 all-to-all-start.4
  556.5 16.8 copy-start.21
  556.5 16.8 copy-start.38
  556.5 17.1 %copy-start.74 = (f32[32,256]{1,0:T(8,128)S(1)}, f32[32,256]{1,0:T(8,128)}, u32[]{:S(2)}) copy-start(f32[32,256]{1,0:T(8,128)} %get-tuple-element.194) | copy-start | bytes 98308
  556.5 17.1 %copy-start.81 = (s32[320]{0:T(512)S(1)}, s32[320]{0:T(512)}, u32[]{:S(2)}) copy-start(s32[320]{0:T(512)} %copy-done.80) | copy-start | bytes 3844
  563.5 9.6 all-to-all-start.2
  575.0 54.9 %all-to-all-start.3 = ((bf16[32,10,256]{2,1,0:T(8,128)(2,1)}), bf16[32,10,256]{2,1,0:T(8,128)(2,1)S(1)}, u32[]{:S(2)}, u32[]{:S(2)}) async-start(bf16[32,10,256]{2,1,0:T(8,128)(2,1)} %convert_element_type.167), calls=%async_computation.4 | async-start | bytes 524288 | tf_op jit(solution)/shard_map/all_to_all | solution.py:322
  581.0 55.1 %copy-start.3 = (f32[3968]{0:T(1024)}, f32[3968]{0:T(1024)S(1)}, u32[]{:S(2)}) copy-start(f32[3968]{0:T(1024)S(1)} %scatter_fusion.1) | copy-start | bytes 47620
  (84 other events, 298.5 us)
Sparse Core Ops, SparseCore 0:
  278.2 134.9 reduce-scatter.12
  493.6 91.8 reduce-scatter.34
  592.0 94.7 reduce-scatter.14
  693.4 97.9 reduce-scatter.28
  797.2 97.9 reduce-scatter.18
  901.8 97.9 reduce-scatter.16
  1005.7 97.9 reduce-scatter.26
  1110.4 98.0 reduce-scatter.24
  1214.4 98.0 reduce-scatter.22
  1319.0 98.0 reduce-scatter.20
  1423.6 134.2 reduce-scatter.30
  1565.3 134.5 reduce-scatter.32
where the time goes:
time: 1710 us
  waiting for transfers between devices  1220 us (71%)
  matrix products  197 us (12%)
  blocking collectives  162 us (9%)
  local copies, waits for them, and re-layouts  50 us (3%)
  other arithmetic  38.8 us (2%)
  starting transfers between devices  19.1 us (1%)
  between operations  18.7 us (1%)
    reduce_scatter x1, waiting for transfers between devices, body(): lax.psum_scatter(down_grad, 'dp', scatter_dimension=0, tiled=True)  142 us
    reduce_scatter x1, waiting for transfers between devices, body(): lax.psum_scatter(up_weight_grad, 'dp', scatter_dimension=0, tiled=True)  141 us
    reduce_scatter x1, waiting for transfers between devices, body(): lax.psum_scatter(head_terms.reshape(total_mask, emb_width), 'dp', scatter...  135 us
    reduce_scatter x1, waiting for transfers between devices, body(): lax.psum_scatter(key_weight_grad, 'dp', scatter_dimension=0, tiled=True)  105 us
    reduce_scatter x1, waiting for transfers between devices, body(): lax.psum_scatter(query_ew_grad, 'dp', scatter_dimension=0, tiled=True)  105 us
    reduce_scatter x1, waiting for transfers between devices, body(): lax.psum_scatter(out_weight_grad, 'dp', scatter_dimension=0, tiled=True)  105 us
    reduce_scatter x1, waiting for transfers between devices, body(): lax.psum_scatter(query_ww_grad, 'dp', scatter_dimension=0, tiled=True)  105 us
    reduce_scatter x1, waiting for transfers between devices, body(): lax.psum_scatter(query_ee_grad, 'dp', scatter_dimension=0, tiled=True)  104 us
  transfers between devices with their start and end apart: 17, of which 15 were waited for; matrix products, arithmetic and copies ran while one was open for 5% of the time, Pallas kernels for 0%

commit v1 on v0

--- a/solution.py
+++ b/solution.py
@@ -1,7 +1,13 @@
+import functools
+
 import jax
 import jax.numpy as jnp
 from jax import lax
+from jax.experimental import pallas as pl
+from jax.experimental.pallas import tpu as pltpu
 from jax.sharding import PartitionSpec as P
+
+MESH_ID = pl.DeviceIdType.MESH
 
 HD = 64
 
@@ -59,6 +65,222 @@
         "qhd,khd->hqk", query_entity, key_rows[word_count:], preferred_element_type=jnp.float32
     )
     return jnp.where(allowed[None], jnp.concatenate([to_words, to_entities], axis=2), MASKED)
+
+
+def greet_all(me, devices):
+    barrier = pltpu.get_barrier_semaphore()
+
+    def greet(step, carry):
+        pl.semaphore_signal(
+            barrier, inc=1, device_id=(lax.rem(me + step, devices),), device_id_type=MESH_ID
+        )
+        return carry
+
+    lax.fori_loop(1, devices, greet, 0)
+    pl.semaphore_wait(barrier, devices - 1)
+
+
+def swap_kernel(devices, gather, source, target, send_sem, recv_sem):
+    me = lax.axis_index("dp")
+    greet_all(me, devices)
+
+    def piece(step):
+        peer = lax.rem(me + step, devices)
+        return pltpu.make_async_remote_copy(
+            src_ref=source if gather else source.at[peer],
+            dst_ref=target.at[me],
+            send_sem=send_sem.at[step],
+            recv_sem=recv_sem.at[step],
+            device_id=(peer,),
+            device_id_type=MESH_ID,
+        )
+
+    def begin(step, carry):
+        piece(step).start()
+        return carry
+
+    def finish(step, carry):
+        piece(step).wait()
+        return carry
+
+    lax.fori_loop(1, devices, begin, 0)
+    target[me] = source[...] if gather else source[me]
+    lax.fori_loop(1, devices, finish, 0)
+
+
+def direct_swap(value, collective_id, gather=False):
+    devices = lax.axis_size("dp")
+    shape = (devices,) + value.shape if gather else value.shape
+    return pl.pallas_call(
+        functools.partial(swap_kernel, devices, gather),
+        out_shape=jax.ShapeDtypeStruct(shape, value.dtype),
+        in_specs=[pl.BlockSpec(memory_space=pltpu.VMEM)],
+        out_specs=pl.BlockSpec(memory_space=pltpu.VMEM),
+        scratch_shapes=[
+            pltpu.SemaphoreType.DMA((devices,)),
+            pltpu.SemaphoreType.DMA((devices,)),
+        ],
+        compiler_params=pltpu.CompilerParams(collective_id=collective_id, has_side_effects=True),
+    )(value)
+
+
+def stage_masks(devices):
+    if devices == 32:
+        axes = [[2], [4], [8, 16]]
+    elif devices == 128:
+        axes = [[2, 4], [8, 16], [32, 64]]
+    else:
+        axes = [[2**bit] for bit in range(1, devices.bit_length() - 1)]
+        axes = axes + [[] for _ in range(3 - len(axes))]
+    first, second, third = axes[0], axes[1], sum(axes[2:], [])
+    return (
+        [1] + first + second + third,
+        [1] + second + first + third,
+        [1] + third + first + second,
+    )
+
+
+def sum_kernel(masks, rows, *refs):
+    parts = len(masks)
+    stages = len(masks[0])
+    sources, results = refs[:parts], refs[parts : 2 * parts]
+    landing = refs[2 * parts : 3 * parts]
+    send_sem, recv_sem = refs[3 * parts :]
+    me = lax.axis_index("dp")
+    barrier = pltpu.get_barrier_semaphore()
+    partner_of = {}
+    for mask in masks[0]:
+        bit = lax.rem(lax.div(me, mask), 2)
+        partner_of[mask] = (me + mask - 2 * mask * bit, bit)
+    for mask in masks[0]:
+        pl.semaphore_signal(
+            barrier, inc=1, device_id=(partner_of[mask][0],), device_id_type=MESH_ID
+        )
+    pl.semaphore_wait(barrier, stages)
+    sizes = [[rows[part] * 2 ** (stages - 1 - stage) for stage in range(stages)] for part in range(parts)]
+    places = [[sum(size[:stage]) for stage in range(stages)] for size in sizes]
+
+    def launch(part, stage):
+        partner, bit = partner_of[masks[part][stage]]
+        size = sizes[part][stage]
+        away = (1 - bit) * size
+        copy = pltpu.make_async_remote_copy(
+            src_ref=sources[part].at[pl.ds(away, size)]
+            if stage == 0
+            else landing[part].at[pl.ds(places[part][stage - 1] + away, size)],
+            dst_ref=landing[part].at[pl.ds(places[part][stage], size)],
+            send_sem=send_sem.at[part, stage],
+            recv_sem=recv_sem.at[part, stage],
+            device_id=(partner,),
+            device_id_type=MESH_ID,
+        )
+        copy.start()
+        return copy
+
+    flying = [launch(part, 0) for part in range(parts)]
+
+    def add_rows(part, stage, start, count):
+        keep = partner_of[masks[part][stage]][1] * sizes[part][stage] + start
+        last = stage == stages - 1
+
+        def step(index, carry):
+            theirs = pl.ds(pl.multiple_of(places[part][stage] + start + index * 16, 16), 16)
+            if stage == 0:
+                mine = sources[part][pl.ds(pl.multiple_of(keep + index * 16, 16), 16)]
+            else:
+                mine = landing[part][
+                    pl.ds(pl.multiple_of(places[part][stage - 1] + keep + index * 16, 16), 16)
+                ]
+            total = mine.astype(jnp.float32) + landing[part][theirs].astype(jnp.float32)
+            if last:
+                results[part][pl.ds(pl.multiple_of(index * 16, 16), 16)] = total
+            else:
+                landing[part][theirs] = total.astype(jnp.bfloat16)
+            return carry
+
+        lax.fori_loop(0, count // 16, step, 0, unroll=min(4, count // 16))
+
+    for stage in range(stages):
+        for part in range(parts):
+            flying[part].wait()
+            if stage == stages - 1:
+                add_rows(part, stage, 0, sizes[part][stage])
+                continue
+            bit = partner_of[masks[part][stage + 1]][1]
+            half = sizes[part][stage] // 2
+            add_rows(part, stage, (1 - bit) * half, half)
+            flying[part] = launch(part, stage + 1)
+            add_rows(part, stage, bit * half, half)
+
+
+def sum_scatter(parts, collective_id):
+    devices = lax.axis_size("dp")
+    masks = stage_masks(devices)
+    rows = [part.shape[1] for part in parts]
+    width = parts[0].shape[2]
+    bits = devices.bit_length() - 1
+    ordered = []
+    for part, order in zip(parts, masks):
+        view = part.reshape((2,) * bits + part.shape[1:])
+        places = [bits - mask.bit_length() for mask in order]
+        view = view.transpose(tuple(places) + (bits, bits + 1))
+        ordered.append(view.reshape(devices * part.shape[1], width))
+    return pl.pallas_call(
+        functools.partial(sum_kernel, masks, rows),
+        out_shape=[jax.ShapeDtypeStruct((count, width), jnp.float32) for count in rows],
+        in_specs=[pl.BlockSpec(memory_space=pltpu.VMEM)] * len(parts),
+        out_specs=[pl.BlockSpec(memory_space=pltpu.VMEM)] * len(parts),
+        scratch_shapes=[pltpu.VMEM((devices * count, width), jnp.bfloat16) for count in rows]
+        + [pltpu.SemaphoreType.DMA((len(parts), bits)), pltpu.SemaphoreType.DMA((len(parts), bits))],
+        input_output_aliases={},
+        compiler_params=pltpu.CompilerParams(
+            collective_id=collective_id, has_side_effects=True, vmem_limit_bytes=56 * 2**20
+        ),
+    )(*ordered)
+
+
+def by_owner(grad, width):
+    devices = lax.axis_size("dp")
+    rows = grad.shape[0] // devices
+    blocks = grad.astype(jnp.bfloat16).reshape(devices, rows, grad.shape[1])
+    if grad.shape[1] > width:
+        cuts = grad.shape[1] // width
+        return jnp.concatenate(jnp.split(blocks, cuts, axis=2), axis=1)
+    if grad.shape[1] < width:
+        return blocks.reshape(devices, rows * grad.shape[1] // width, width)
+    return blocks
+
+
+def from_owner(rows, shape):
+    devices = lax.axis_size("dp")
+    count, width = shape[0] // devices, shape[1]
+    if width > rows.shape[1]:
+        return jnp.concatenate(jnp.split(rows, width // rows.shape[1], axis=0), axis=1)
+    return rows.reshape(count, width)
+
+
+def sum_all(groups, collective_id):
+    width = groups[0][0].shape[1]
+    width = min(grad.shape[1] for group in groups for grad in group if grad.shape[1] >= 768)
+    devices = lax.axis_size("dp")
+    packed = []
+    for group in groups:
+        pieces = [by_owner(grad, width) for grad in group]
+        count = sum(piece.shape[1] for piece in pieces)
+        room = -(-count // 16) * 16 - count
+        if room:
+            pieces.append(jnp.zeros((devices, room, width), jnp.bfloat16))
+        packed.append(jnp.concatenate(pieces, axis=1))
+    sums = sum_scatter(packed, collective_id)
+    results = []
+    for group, total in zip(groups, sums):
+        place, outs = 0, []
+        for grad in group:
+            count = grad.shape[0] // devices * grad.shape[1] // width
+            outs.append(from_owner(total[place : place + count], grad.shape))
+            place += count
+        results.append(outs)
+    return results
 
 
 def body(
@@ -103,11 +325,17 @@
     table_rows = entity_table.shape[0]
     total_mask = mask_count * devices
     grad_scale = 1.0 / total_mask
-    asked_ids = lax.all_to_all(request_rows, "dp", split_axis=0, concat_axis=0, tiled=True)
+    id_block = jnp.pad(request_rows[:, None, :], ((0, 0), (0, 7), (0, 128 - capacity)))
+    asked_ids = direct_swap(id_block, 0)[:, 0, :capacity]
     found_rows = jnp.take(entity_table, asked_ids, axis=0)
     found_bias = jnp.take(vocab_bias, asked_ids, axis=0)
-    back_rows = lax.all_to_all(found_rows, "dp", split_axis=0, concat_axis=0, tiled=True)
-    back_bias = lax.all_to_all(found_bias, "dp", split_axis=0, concat_axis=0, tiled=True)
+    cap_room = -(-capacity // 16) * 16 - capacity
+    found_all = jnp.concatenate(
+        [found_rows, jnp.broadcast_to(found_bias[:, :, None], found_bias.shape + (128,))], axis=2
+    )
+    back_all = direct_swap(jnp.pad(found_all, ((0, 0), (0, cap_room), (0, 0))), 1)
+    back_rows = back_all[:, :capacity, :emb_width]
+    back_bias = back_all[:, :capacity, emb_width]
     got_rows = back_rows
     got_bias = back_bias
     slot_ids = request_slot.reshape(devices * capacity)
@@ -169,7 +397,7 @@
     head_low = head_act(head_pre, head_gain, head_bias).astype(jnp.bfloat16)
     head_f32 = head_low.astype(jnp.float32)
     target_logit = jnp.sum(head_f32 * target_vecs, axis=1) + target_bias
-    all_heads = lax.all_gather(head_low, "dp", axis=0, tiled=True)
+    all_heads = direct_swap(head_low, 2, gather=True).reshape(total_mask, emb_width)
     block_rows = min(512, total_mask)
     block_count = total_mask // block_rows
     bias_f32 = vocab_bias.astype(jnp.float32)
@@ -187,10 +415,20 @@
     local_top = local_top.reshape(total_mask)
     local_total = local_total.reshape(total_mask)
     target_sum = jnp.sum(target_logit)
-    global_top = lax.pmax(local_top, "dp")
-    global_total, target_total = lax.psum(
-        (local_total * jnp.exp(local_top - global_top), target_sum), "dp"
-    )
+    stats = jnp.concatenate(
+        [
+            local_top.reshape(total_mask // 128, 128),
+            local_total.reshape(total_mask // 128, 128),
+            jnp.full((8, 128), target_sum),
+        ],
+        axis=0,
+    )
+    all_stats = direct_swap(stats, 3, gather=True)
+    all_tops = all_stats[:, : total_mask // 128].reshape(devices, total_mask)
+    all_totals = all_stats[:, total_mask // 128 : total_mask // 64].reshape(devices, total_mask)
+    target_total = jnp.sum(all_stats[:, total_mask // 64, 0])
+    global_top = jnp.max(all_tops, axis=0)
+    global_total = jnp.sum(all_totals * jnp.exp(all_tops - global_top[None, :]), axis=0)
     lse_all = global_top + jnp.log(global_total)
     loss_value = (jnp.sum(lse_all) - target_total) * grad_scale
     own_lse = lax.dynamic_slice_in_dim(lse_all, lax.axis_index("dp") * mask_count, mask_count, 0)
@@ -212,9 +450,8 @@
     (table_grad, bias_grad), head_terms = lax.scan(
         block_back, start_grads, jnp.arange(block_count, dtype=jnp.int32)
     )
-    head_grad = lax.psum_scatter(
-        head_terms.reshape(total_mask, emb_width), "dp", scatter_dimension=0, tiled=True
-    )
+    head_parts = direct_swap(head_terms.reshape(devices, mask_count, emb_width), 4)
+    head_grad = jnp.sum(head_parts, axis=0)
     head_grad = head_grad - grad_scale * target_vecs
     target_grad = -grad_scale * head_f32
     pre_grad, head_gain_grad, head_bias_grad = jax.vjp(head_act, head_pre, head_gain, head_bias)[1](
@@ -318,22 +555,19 @@
     placing_f32 = placing.astype(jnp.float32)
     per_request = dot_exact(placing_f32.T, vec_grad)
     bias_request = dot_exact(placing_f32.T, bias_vec_grad[:, None])[:, 0]
-    back_rows, back_bias = (
-        lax.all_to_all(
+    back_block = jnp.concatenate(
+        [
             per_request.reshape(devices, capacity, emb_width).astype(jnp.bfloat16),
-            "dp",
-            split_axis=0,
-            concat_axis=0,
-            tiled=True,
-        ).astype(jnp.float32),
-        lax.all_to_all(
-            bias_request.reshape(devices, capacity).astype(jnp.bfloat16),
-            "dp",
-            split_axis=0,
-            concat_axis=0,
-            tiled=True,
-        ).astype(jnp.float32),
-    )
+            jnp.broadcast_to(
+                bias_request.reshape(devices, capacity, 1).astype(jnp.bfloat16),
+                (devices, capacity, 128),
+            ),
+        ],
+        axis=2,
+    )
+    back_block = direct_swap(jnp.pad(back_block, ((0, 0), (0, cap_room), (0, 0))), 5)
+    back_rows = back_block[:, :capacity, :emb_width].astype(jnp.float32)
+    back_bias = back_block[:, :capacity, emb_width].astype(jnp.float32)
     flat_ids = asked_ids.reshape(devices * capacity)
     table_grad = table_grad + jax.ops.segment_sum(
         back_rows.reshape(devices * capacity, emb_width), flat_ids, num_segments=table_rows
@@ -341,26 +575,48 @@
     bias_grad = bias_grad + jax.ops.segment_sum(
         back_bias.reshape(devices * capacity), flat_ids, num_segments=table_rows
     )
-    all_sums = tuple(
-        (
-            lax.psum_scatter(head_weight_grad, "dp", scatter_dimension=0, tiled=True),
-            lax.psum_scatter(head_gain_grad, "dp", scatter_dimension=0, tiled=True),
-            lax.psum_scatter(head_bias_grad, "dp", scatter_dimension=0, tiled=True),
-            lax.psum_scatter(norm2_gain_grad, "dp", scatter_dimension=0, tiled=True),
-            lax.psum_scatter(norm2_bias_grad, "dp", scatter_dimension=0, tiled=True),
-            lax.psum_scatter(up_weight_grad, "dp", scatter_dimension=0, tiled=True),
-            lax.psum_scatter(down_grad, "dp", scatter_dimension=0, tiled=True),
-            lax.psum_scatter(norm1_gain_grad, "dp", scatter_dimension=0, tiled=True),
-            lax.psum_scatter(norm1_bias_grad, "dp", scatter_dimension=0, tiled=True),
-            lax.psum_scatter(out_weight_grad, "dp", scatter_dimension=0, tiled=True),
-            lax.psum_scatter(query_ww_grad, "dp", scatter_dimension=0, tiled=True),
-            lax.psum_scatter(query_we_grad, "dp", scatter_dimension=0, tiled=True),
-            lax.psum_scatter(query_ew_grad, "dp", scatter_dimension=0, tiled=True),
-            lax.psum_scatter(query_ee_grad, "dp", scatter_dimension=0, tiled=True),
-            lax.psum_scatter(key_weight_grad, "dp", scatter_dimension=0, tiled=True),
-            lax.psum_scatter(value_weight_grad, "dp", scatter_dimension=0, tiled=True),
-            lax.psum_scatter(dense_grad, "dp", scatter_dimension=0, tiled=True),
-        )
+    vectors = [
+        head_gain_grad,
+        head_bias_grad,
+        norm2_gain_grad,
+        norm2_bias_grad,
+        norm1_gain_grad,
+        norm1_bias_grad,
+    ]
+    cuts = [vector.reshape(devices, -1) for vector in vectors]
+    spots = [0]
+    for cut in cuts:
+        spots.append(spots[-1] + cut.shape[1])
+    block = jnp.concatenate(cuts, axis=1)
+    block = jnp.pad(block, ((0, 0), (0, 128 - spots[-1])))[:, None, :]
+    vector_sums = jnp.sum(direct_swap(jnp.pad(block, ((0, 0), (0, 7), (0, 0))), 6)[:, 0], axis=0)
+    vector_out = [vector_sums[spots[i] : spots[i + 1]] for i in range(len(cuts))]
+    sums = sum_all(
+        [
+            [up_weight_grad, out_weight_grad, head_weight_grad],
+            [down_grad, query_ww_grad, dense_grad],
+            [query_we_grad, query_ew_grad, query_ee_grad, key_weight_grad, value_weight_grad],
+        ],
+        7,
+    )
+    all_sums = (
+        sums[0][2],
+        vector_out[0],
+        vector_out[1],
+        vector_out[2],
+        vector_out[3],
+        sums[0][0],
+        sums[1][0],
+        vector_out[4],
+        vector_out[5],
+        sums[0][1],
+        sums[1][1],
+        sums[2][0],
+        sums[2][1],
+        sums[2][2],
+        sums[2][3],
+        sums[2][4],
+        sums[1][2],
     )
     return (
         loss_value,

time: 1710 us -> 596 us (0.35)
  waiting for transfers between devices: 1220 us -> 0 us
  Pallas kernels: 0 us -> 246 us
  blocking collectives: 162 us -> 0 us
  local copies, waits for them, and re-layouts: 50 us -> 80.6 us
  starting transfers between devices: 19.1 us -> 0 us
  other arithmetic: 38.8 us -> 56.1 us
    reduce_scatter x12 -> x0, waiting for transfers between devices: 1200 us -> none  [the longest x1 142 us: body(): lax.psum_scatter(down_grad, 'dp', scatter_dimension=0, tiled=True)]
    pallas_call x0 -> x8, Pallas kernels: none -> 246 us  [the longest x1 123 us: sum_scatter(): pl.pallas_call(functools.partial(sum_kernel, masks, rows), out_shape=[jax...]
    psum x2 -> x0, blocking collectives: 82.4 us -> none  [body(): lax.psum((local_total * jnp.exp(local_top - global_top), target_sum), 'dp')]
    all_gather x1 -> x0, blocking collectives: 42.4 us -> none  [body(): all_heads = lax.all_gather(head_low, 'dp', axis=0, tiled=True)]
    pmax x1 -> x0, blocking collectives: 36.9 us -> none  [body(): global_top = lax.pmax(local_top, 'dp')]
    all_to_all x5 -> x0, waiting for transfers between devices: 21.3 us -> none  [the longest x1 9.45 us: body(): lax.all_to_all(found_rows, 'dp', split_axis=0, concat_axis=0, tiled=True)]
    dot_general x13, matrix products: 51.4 us -> 31.1 us  [dot_left_t(): lax.dot_general(left_side, right_side, (((0,), (0,)), ((), ())), preferre...]
    all_to_all x5 -> x0, starting transfers between devices: 18.4 us -> none  [the longest x1 7.3 us: body(): lax.all_to_all(request_rows, 'dp', split_axis=0, concat_axis=0, tiled=True)]
  transfers between devices with their start and end apart: 17 -> 0, of which waited for: 15 -> 0; matrix products, arithmetic and copies ran while one was open for 5% -> 0% of each run, Pallas kernels for 0% -> 0%
where the time goes in v1:
time: 596 us; the launch traced here: 586 us
  Pallas kernels  246 us (41%)
  matrix products  195 us (33%)
  local copies, waits for them, and re-layouts  80.6 us (14%)
  other arithmetic  56.1 us (9%)
    pallas_call x1, Pallas kernels, sum_scatter(): pl.pallas_call(functools.partial(sum_kernel, masks, rows), out_shape=[jax...  123 us
    pallas_call x7, Pallas kernels, direct_swap(): pl.pallas_call(functools.partial(swap_kernel, devices, gather), out_shape...  123 us
    dot_general x15, matrix products, dot_right_t(): lax.dot_general(left_side, right_side, (((1,), (1,)), ((), ())), preferre...  50.6 us
    dot_general x15, matrix products, dot_plain(): return jnp.dot(left_side, right_side, preferred_element_type=jnp.float32)  48.7 us
    dot_general x13, matrix products, dot_left_t(): lax.dot_general(left_side, right_side, (((0,), (0,)), ((), ())), preferre...  31.1 us
    sub x1, matrix products, body(): score_grad = (attn_prob * (prob_grad - row_delta)).astype(jnp.bfloat16)  24.4 us
    unnamed x216, local copies, waits for them, and re-layouts  23.7 us

profile of v1, /device:TPU:0, one launch (start us, length us, event | category | flops | bytes accessed | tf_op | source)
XLA Modules:
  0.0 585.6 jit_solution(6067891520374630602)
XLA Ops:
  2.2 12.2 %shard_map.425 = s32[32,8,128]{2,1,0:T(8,128)} custom-call(s32[32,8,128]{2,1,0:T(8,128)} %pad.20.source), custom_call_target="tpu_custom_call" | custom-call | tf_op jit(solution)/shard_map/pallas_call | solution.py:114
  16.1 2.5 gather_fusion.1
  23.6 14.8 %shard_map.426 = bf16[32,16,384]{2,1,0:T(8,128)(2,1)} custom-call(bf16[32,16,384]{2,1,0:T(8,128)(2,1)} %fusion.85.source), custom_call_target="tpu_custom_call" | custom-call | tf_op jit(solution)/shard_map/pallas_call | solution.py:114
  51.2 2.5 convolution_convert_fusion.6
  58.4 2.5 fusion.81
  62.1 2.7 fusion.115
  65.7 2.3 copy.84
  70.0 2.5 fusion.83
  72.6 2.2 fusion.118
  76.8 3.5 copy-done.4
  80.3 3.4 fusion.10
  83.8 9.8 %fusion.46 = bf16[12,64,640]{2,1,0:T(8,128)(2,1)} fusion(bf16[640,12,64]{0,2,1:T(8,128)(2,1)} %bitcast.199, f32[12,640]{1,0:T(8,128)S(1)} %fusion.10, f32[12,640]{1,0:T(8,128)S(1)} %fusion.144, f32[12,640,128]{1,2,0:T(8,128)S(1)} %copy-done.6, f32[12,640,512]{1,2,0:T(8,128)} %copy-done.4, pred[640,640]{0,1:T(8,128)(4,1)S(1)} %broadcast_compare_fusion), kind=kOutput, calls=%fused_computation.99 | convolution fusion | flops 654213120 | bytes 22097920 | tf_op jit(solution)/shard_map/hqk,khd->qhd/dot_general | solution.py:381
  93.7 2.4 fusion.157
  96.6 24.0 %multiply_convert_fusion.2 = (bf16[640,3072]{1,0:T(8,128)(2,1)S(1)}, f32[640,3072]{1,0:T(8,128)}, f32[640,3072]{1,0:T(8,128)}) fusion(bf16[768,3072]{1,0:T(8,128)(2,1)} %param.48, f32[640,768]{1,0:T(8,128)S(1)} %get-tuple-element.238, f32[768]{0:T(1024)S(1)} %copy-done.93, f32[768]{0:T(1024)S(1)} %copy-done.76, f32[640]{0:T(1024)S(1)} %fusion.125, ...), kind=kOutput, calls=%fused_computation.36 | convolution fusion | flops 3150151680 | bytes 26356736 | tf_op jit(solution)/shard_map/dot_general | solution.py:20
  120.7 3.4 fusion.158
  127.7 18.3 %shard_map.427 = bf16[32,32,256]{2,1,0:T(8,128)(2,1)} custom-call(bf16[32,256]{1,0:T(8,128)(2,1)} %get-tuple-element.194.source), custom_call_target="tpu_custom_call" | custom-call | tf_op jit(solution)/shard_map/pallas_call | solution.py:114
  146.0 23.0 %while.27 = (s32[]{:T(128)}, f32[2,512]{1,0:T(2,128)S(1)}, f32[2,512]{1,0:T(2,128)S(1)}, s32[2]{0:T(128)S(1)}, bf16[1024,256]{1,0:T(8,128)(2,1)}, /*index=5*/bf1...) while((s32[]{:T(128)}, f32[2,512]{1,0:T(2,128)S(1)}, ...), condition=%wide.region_11.12_spmd, body=%wide.region_8.11_spmd.sunk | while | flops 1050344448 | bytes 18592956 | solution.py:414
  147.3 5.4 add_reduce_fusion.2
  152.7 4.8 exponential_reduce_fusion.2
  158.8 5.4 add_reduce_fusion.2
  164.2 4.8 exponential_reduce_fusion.2
  173.3 16.8 %shard_map.428 = f32[32,24,128]{2,1,0:T(8,128)} custom-call(f32[24,128]{1,0:T(8,128)} %maximum_maximum_fusion.source), custom_call_target="tpu_custom_call" | custom-call | tf_op jit(solution)/shard_map/pallas_call | solution.py:114
  196.1 29.7 %while.28 = (s32[]{:T(128)}, f32[3968,256]{1,0:T(8,128)}, f32[3968]{0:T(1024)S(1)}, f32[2,512,256]{2,1,0:T(8,128)}, s32[2]{0:T(128)S(1)}, /*index=5*/bf16[1024,2...) while((s32[]{:T(128)}, f32[3968,256]{1,0:T(8,128)}, ...), condition=%wide.region_20.21_spmd.clone, body=%wide.region_18.20_spmd.clone.sunk | while | flops 3134787584 | bytes 50155308 | solution.py:450
  197.5 5.0 convert_reduce_fusion.3
  202.5 5.5 convolution_add_fusion.3
  211.6 5.0 convert_reduce_fusion.3
  216.7 6.8 %convolution_add_fusion.3 = f32[3968,256]{1,0:T(8,128)} fusion(bf16[512,3968]{1,0:T(8,128)(2,1)} %get-tuple-element.353, f32[3968,256]{1,0:T(8,128)} %get-tuple-element.402, pred[]{:T(512)S(6)} %compare.30, bf16[1024,256]{1,0:T(8,128)(2,1)} %get-tuple-element.419, s32[]{:T(128)S(6)} %select_n.84), kind=kOutput, calls=%fused_computation.11.clone.1 | convolution fusion | flops 1042219008 | bytes 12451845 | tf_op jit(solution)/shard_map/while/body/eval_jaxpr/dot_general | solution.py:24
  225.8 27.5 %shard_map.429 = f32[32,32,256]{2,1,0:T(8,128)} custom-call(f32[32,32,256]{2,1,0:T(8,128)} %bitcast.198), custom_call_target="tpu_custom_call" | custom-call | tf_op jit(solution)/shard_map/pallas_call | solution.py:114
  258.6 2.6 multiply_reduce_fusion.2
  262.1 10.9 %add_convert_fusion = bf16[640,3072]{1,0:T(8,128)(2,1)S(1)} fusion(f32[640,3072]{1,0:T(8,128)} %get-tuple-element.206, f32[640,3072]{1,0:T(8,128)} %get-tuple-element.239, bf16[3072,768]{1,0:T(8,128)(2,1)} %param.49, f32[640,768]{1,0:T(8,128)S(1)} %get-tuple-element.198, f32[640]{0:T(1024)S(1)} %negate_multiply_fusion.3), kind=kOutput, calls=%fused_computation.35 | convolution fusion | flops 3048407040 | bytes 26348032 | tf_op jit(solution)/shard_map/dot_general | solution.py:30
  273.0 4.3 multiply_reduce_fusion.1
  282.0 2.3 copy.89
  284.2 24.4 %multiply_convert_fusion.1 = bf16[12,640,640]{1,2,0:T(8,128)(2,1)} fusion(f32[12,640]{1,0:T(8,128)} %log_add_fusion, bf16[640,12,64]{0,2,1:T(8,128)(2,1)} %bitcast.203, bf16[640,12,64]{0,2,1:T(8,128)(2,1)} %bitcast.200, f32[12,640,128]{1,2,0:T(8,128)} %fusion.115, f32[12,640,512]{1,2,0:T(8,128)} %copy-done.4, pred[640,640]{0,1:T(8,128)(4,1)} %copy-done.20), kind=kOutput, calls=%fused_computation.21 | convolution fusion | flops 1307451520 | bytes 31897600 | tf_op jit(solution)/shard_map/sub | solution.py:494
  308.7 3.1 fusion.72
  311.8 5.9 %fusion.65 = bf16[512,12,64]{0,2,1:T(8,128)(2,1)S(1)} fusion(bf16[12,640,640]{1,2,0:T(8,128)(2,1)} %multiply_convert_fusion.1, f32[128,12,64]{0,2,1:T(8,128)S(1)} %bitcast.192, f32[512,12,64]{0,2,1:T(8,128)S(1)} %bitcast.186), kind=kOutput, calls=%fused_computation.109 | convolution fusion | flops 505184256 | bytes 10616832 | tf_op jit(solution)/shard_map/hqk,qhd->khd/dot_general | solution.py:511
  318.8 2.3 fusion.162
  327.9 10.2 %fusion.47 = bf16[12,64,640]{2,1,0:T(8,128)(2,1)} fusion(bf16[640,12,64]{0,2,1:T(8,128)(2,1)} %bitcast.204, f32[12,640]{1,0:T(8,128)} %log_add_fusion, f32[12,640,128]{1,2,0:T(8,128)} %fusion.115, f32[12,640,512]{1,2,0:T(8,128)} %copy-done.4, pred[640,640]{0,1:T(8,128)(4,1)} %copy-done.20), kind=kOutput, calls=%fused_computation.100 | convolution fusion | flops 649297920 | bytes 22067200 | tf_op jit(solution)/shard_map/hqk,qhd->khd/dot_general | solution.py:489
  338.1 4.2 fusion.33
  357.8 20.2 %shard_map.430 = bf16[32,16,384]{2,1,0:T(8,128)(2,1)} custom-call(bf16[32,16,384]{2,1,0:T(8,128)(2,1)} %fusion.86.source), custom_call_target="tpu_custom_call" | custom-call | tf_op jit(solution)/shard_map/pallas_call | solution.py:114
  381.6 6.8 %scatter_fusion = f32[3968,256]{1,0:T(8,128)} fusion(f32[3968,256]{1,0:T(8,128)} %get-tuple-element.116, s32[320]{0:T(512)} %reshape.438, f32[320,256]{1,0:T(8,128)} %reshape.440), kind=kCustom, calls=%fused_computation.2 | custom fusion | flops 81920 | bytes 984320 | tf_op jit(solution)/shard_map/scatter-add | solution.py:572
  391.5 3.4 scatter_fusion.1
  394.9 6.6 %convolution_convert_fusion.1 = bf16[768,3072]{1,0:T(8,128)(2,1)S(1)} fusion(bf16[640,3072]{1,0:T(8,128)(2,1)} %copy-done.95, f32[640,768]{1,0:T(8,128)S(1)} %copy-done.11, f32[768]{0:T(1024)} %param.47, f32[768]{0:T(1024)} %param.46, f32[640]{0:T(1024)} %copy-done.70, f32[640]{0:T(1024)} %copy-done.62), kind=kOutput, calls=%fused_computation.56 | convolution fusion | flops 3024715776 | bytes 10628096 | tf_op jit(solution)/shard_map/dot_general | solution.py:24
  410.1 6.3 %copy.96 = bf16[2,2,2,2,2,128,768]{6,5,4,3,2,1,0:T(8,128)(2,1)} copy(bf16[2,2,2,2,2,128,768]{6,5,0,1,2,3,4:T(8,128)(2,1)} %bitcast.43) | data formatting | bytes 12582912 | tf_op jit(solution)/shard_map/transpose | solution.py:226
  418.6 4.4 convolution_convert_fusion
  423.9 3.0 copy.117
  431.9 2.6 copy-done.9
  434.5 123.1 %shard_map.431 = (f32[128,768]{1,0:T(8,128)}, f32[128,768]{1,0:T(8,128)}, f32[128,768]{1,0:T(8,128)}) custom-call(bf16[4096,768]{1,0:T(8,128)(2,1)} %bitcast.162, bf16[4096,768]{1,0:T(8,128)(2,1)} %bitcast.163, bf16[4096,768]{1,0:T(8,128)(2,1)} %bitcast.165), custom_call_target="tpu_custom_call" | custom-call | tf_op jit(solution)/shard_map/pallas_call | solution.py:228
  563.7 13.1 %shard_map.432 = f32[32,8,128]{2,1,0:T(8,128)} custom-call(f32[32,8,128]{2,1,0:T(8,128)} %pad.24.source), custom_call_target="tpu_custom_call" | custom-call | tf_op jit(solution)/shard_map/pallas_call | solution.py:114
  (382 shorter events, 121.9 us)
Async XLA Ops:
  0.7 93.0 %copy-start = (bf16[768,768]{1,0:T(8,128)(2,1)S(1)}, bf16[768,768]{1,0:T(8,128)(2,1)}, u32[]{:S(2)}) copy-start(bf16[768,768]{1,0:T(8,128)(2,1)} %param.45) | copy-start | bytes 3538948
  0.7 15.4 %copy-start.1 = (bf16[3968]{0:T(1024)(128)(2,1)S(1)}, bf16[3968]{0:T(1024)(128)(2,1)}, u32[]{:S(2)}) copy-start(bf16[3968]{0:T(1024)(128)(2,1)} %param.37) | copy-start | bytes 23812
  18.6 21.5 %copy-start.74 = (s32[32,10]{0,1:T(8,128)S(1)}, s32[32,10]{0,1:T(8,128)}, u32[]{:S(2)}) copy-start(s32[32,10]{0,1:T(8,128)} %param.34) | copy-start | bytes 3844
  40.2 8.8 %copy-start.58 = (s32[32,10]{1,0:T(8,128)}, s32[32,10]{1,0:T(8,128)S(1)}, u32[]{:S(2)}) copy-start(s32[32,10]{1,0:T(8,128)S(1)} %copy.79) | copy-start | bytes 3844
  40.3 8.6 %copy-start.65 = (s32[320]{0:T(512)}, s32[320]{0:T(512)S(1)}, u32[]{:S(2)}) copy-start(s32[320]{0:T(512)S(1)} %eq.59) | copy-start | bytes 3844
  40.3 6.7 %copy-start.43 = (bf16[768,768]{1,0:T(8,128)(2,1)S(1)}, bf16[768,768]{1,0:T(8,128)(2,1)}, u32[]{:S(2)}) copy-start(bf16[768,768]{1,0:T(8,128)(2,1)} %param.44) | copy-start | bytes 3538948
  56.4 8.4 %copy-start.29 = (bf16[128,768]{0,1:T(8,128)(2,1)}, bf16[128,768]{0,1:T(8,128)(2,1)S(1)}, u32[]{:S(2)}) copy-start(bf16[128,768]{0,1:T(8,128)(2,1)S(1)} %copy.87) | copy-start | bytes 589828
  58.4 6.3 %copy-start.33 = (f32[128,768]{0,1:T(8,128)}, f32[128,768]{0,1:T(8,128)S(1)}, u32[]{:S(2)}) copy-start(f32[128,768]{0,1:T(8,128)S(1)} %fusion.100) | copy-start | bytes 1179652
  75.2 8.5 %copy-start.20 = (pred[640,640]{0,1:T(8,128)(4,1)}, pred[640,640]{0,1:T(8,128)(4,1)S(1)}, u32[]{:S(2)}) copy-start(pred[640,640]{0,1:T(8,128)(4,1)S(1)} %broadcast_compare_fusion) | copy-start | bytes 1228804
  83.8 9.9 %copy-start.15 = (f32[512,768]{1,0:T(8,128)S(1)}, f32[512,768]{1,0:T(8,128)}, u32[]{:S(2)}) copy-start(f32[512,768]{1,0:T(8,128)} %copy-done.14) | copy-start | bytes 4718596
  83.8 9.9 %copy-start.37 = (f32[128,768]{1,0:T(8,128)S(1)}, f32[128,768]{1,0:T(8,128)}, u32[]{:S(2)}) copy-start(f32[128,768]{1,0:T(8,128)} %copy-done.36) | copy-start | bytes 1179652
  93.7 26.9 %slice-start.3 = ((s8[4718592]{0:T(1024)(128)(4,1)}), s8[4194304]{0:T(1024)(128)(4,1)S(1)}, s32[]{:S(2)}) async-start(s8[4718592]{0:T(1024)(128)(4,1)} %bitcast.224), calls=%async_computation.3 | async-start | bytes 8388608
  96.1 24.5 %copy-start.10 = (f32[640,768]{1,0:T(8,128)}, f32[640,768]{1,0:T(8,128)S(1)}, u32[]{:S(2)}) copy-start(f32[640,768]{1,0:T(8,128)S(1)} %get-tuple-element.238) | copy-start | bytes 5898244
  96.2 181.2 %copy-start.62 = (f32[640]{0:T(1024)}, f32[640]{0:T(1024)S(1)}, u32[]{:S(2)}) copy-start(f32[640]{0:T(1024)S(1)} %broadcast_multiply_fusion.1) | copy-start | bytes 7684
  96.5 24.1 %copy-start.63 = (f32[640]{0:T(1024)}, f32[640]{0:T(1024)S(1)}, u32[]{:S(2)}) copy-start(f32[640]{0:T(1024)S(1)} %multiply_reduce_fusion.6) | copy-start | bytes 7684
  96.6 180.8 %copy-start.70 = (f32[640]{0:T(1024)}, f32[640]{0:T(1024)S(1)}, u32[]{:S(2)}) copy-start(f32[640]{0:T(1024)S(1)} %fusion.125) | copy-start | bytes 7684
  96.6 24.0 %slice-start.4 = ((s8[4718592]{0:T(1024)(128)(4,1)}), s8[524288]{0:T(1024)(128)(4,1)S(1)}, s32[]{:S(2)}) async-start(s8[4718592]{0:T(1024)(128)(4,1)} %bitcast.224), calls=%async_computation.4 | async-start | bytes 1048576
  146.0 23.1 %copy-start.59 = (bf16[32,256]{1,0:T(8,128)(2,1)S(1)}, bf16[32,256]{1,0:T(8,128)(2,1)}, u32[]{:S(2)}) copy-start(bf16[32,256]{1,0:T(8,128)(2,1)} %get-tuple-element.194.source) | copy-start | bytes 49156
  146.0 25.1 %copy-start.66 = (s32[320]{0:T(512)S(1)}, s32[320]{0:T(512)}, u32[]{:S(2)}) copy-start(s32[320]{0:T(512)} %copy-done.65) | copy-start | bytes 3844
  169.9 26.2 %copy-start.83 = (f32[32]{0:T(128)}, f32[32]{0:T(128)S(1)}, u32[]{:S(2)}) copy-start(f32[32]{0:T(128)S(1)} %fusion.107) | copy-start | bytes 388
  216.7 6.8 %copy-start.3 = (bf16[512,3968]{1,0:T(8,128)(2,1)S(1)}, bf16[512,3968]{1,0:T(8,128)(2,1)}, u32[]{:S(2)}) copy-start(bf16[512,3968]{1,0:T(8,128)(2,1)} %get-tuple-element.353) | copy-start | bytes 12189700 | tf_op jit(solution)/shard_map/while
  216.7 6.8 %copy-start.44 = (f32[2,512,256]{2,1,0:T(8,128)S(1)}, f32[2,512,256]{2,1,0:T(8,128)}, u32[]{:S(2)}) copy-start(f32[2,512,256]{2,1,0:T(8,128)} %get-tuple-element.404) | copy-start | bytes 3145732 | tf_op jit(solution)/shard_map/while
  225.8 35.4 %copy-start.60 = (f32[1024]{0:T(1024)}, f32[1024]{0:T(1024)S(1)}, u32[]{:S(2)}) copy-start(f32[1024]{0:T(1024)S(1)} %get-tuple-element.430) | copy-start | bytes 12292
  225.8 32.7 %copy-start.8 = (f32[640,768]{1,0:T(8,128)S(1)}, f32[640,768]{1,0:T(8,128)}, u32[]{:S(2)}) copy-start(f32[640,768]{1,0:T(8,128)} %copy-done.7) | copy-start | bytes 5898244
  254.6 6.6 %copy-start.19 = (bf16[640,768]{1,0:T(8,128)(2,1)S(1)}, bf16[640,768]{1,0:T(8,128)(2,1)}, u32[]{:S(2)}) copy-start(bf16[640,768]{1,0:T(8,128)(2,1)} %param.55) | copy-start | bytes 2949124
  261.2 11.8 %slice-start.5 = ((s8[4718592]{0:T(1024)(128)(4,1)}), s8[4194304]{0:T(1024)(128)(4,1)S(1)}, s32[]{:S(2)}) async-start(s8[4718592]{0:T(1024)(128)(4,1)} %bitcast.226), calls=%async_computation.5 | async-start | bytes 8388608
  262.0 11.0 %copy-start.27 = (f32[640,768]{1,0:T(8,128)}, f32[640,768]{1,0:T(8,128)S(1)}, u32[]{:S(2)}) copy-start(f32[640,768]{1,0:T(8,128)S(1)} %get-tuple-element.198) | copy-start | bytes 5898244
  262.0 11.0 %copy-start.81 = (f32[640]{0:T(1024)}, f32[640]{0:T(1024)S(1)}, u32[]{:S(2)}) copy-start(f32[640]{0:T(1024)S(1)} %negate_multiply_fusion.3) | copy-start | bytes 7684
  262.0 11.0 %copy-start.11 = (f32[640,768]{1,0:T(8,128)S(1)}, f32[640,768]{1,0:T(8,128)}, u32[]{:S(2)}) copy-start(f32[640,768]{1,0:T(8,128)} %copy-done.10) | copy-start | bytes 5898244
  262.0 11.0 %slice-start.6 = ((s8[4718592]{0:T(1024)(128)(4,1)}), s8[524288]{0:T(1024)(128)(4,1)S(1)}, s32[]{:S(2)}) async-start(s8[4718592]{0:T(1024)(128)(4,1)} %bitcast.226), calls=%async_computation.6 | async-start | bytes 1048576
  284.2 24.4 %copy-start.34 = (f32[128,768]{0,1:T(8,128)S(1)}, f32[128,768]{0,1:T(8,128)}, u32[]{:S(2)}) copy-start(f32[128,768]{0,1:T(8,128)} %copy-done.33) | copy-start | bytes 1179652
  308.7 12.4 %slice-start = ((s8[9830400]{0:T(1024)(128)(4,1)}), s8[4194304]{0:T(1024)(128)(4,1)S(1)}, s32[]{:S(2)}) async-start(s8[9830400]{0:T(1024)(128)(4,1)} %bitcast.210), calls=%async_computation | async-start | bytes 8388608
  311.8 7.0 %copy-start.91 = (bf16[768,768]{1,0:T(8,128)(2,1)S(1)}, bf16[768,768]{1,0:T(8,128)(2,1)}, u32[]{:S(2)}) copy-start(bf16[768,768]{1,0:T(8,128)(2,1)} %param.43) | copy-start | bytes 3538948
  311.8 9.3 %slice-start.1 = ((s8[9830400]{0:T(1024)(128)(4,1)}), s8[4194304]{0:T(1024)(128)(4,1)S(1)}, s32[]{:S(2)}) async-start(s8[9830400]{0:T(1024)(128)(4,1)} %bitcast.210), calls=%async_computation.1 | async-start | bytes 8388608
  311.8 9.3 %slice-start.2 = ((s8[9830400]{0:T(1024)(128)(4,1)}), s8[1441792]{0:T(1024)(128)(4,1)S(1)}, s32[]{:S(2)}) async-start(s8[9830400]{0:T(1024)(128)(4,1)} %bitcast.210), calls=%async_computation.2 | async-start | bytes 2883584
  327.9 10.2 %copy-start.72 = (f32[640]{0:T(1024)S(1)}, f32[640]{0:T(1024)}, u32[]{:S(2)}) copy-start(f32[640]{0:T(1024)} %copy-done.71) | copy-start | bytes 7684
  394.9 6.6 %copy-start.2 = (f32[3968]{0:T(1024)}, f32[3968]{0:T(1024)S(1)}, u32[]{:S(2)}) copy-start(f32[3968]{0:T(1024)S(1)} %scatter_fusion.1) | copy-start | bytes 47620
  410.1 7.6 %copy-start.22 = (bf16[640,768]{1,0:T(8,128)(2,1)S(1)}, bf16[640,768]{1,0:T(8,128)(2,1)}, u32[]{:S(2)}) copy-start(bf16[640,768]{1,0:T(8,128)(2,1)} %copy-done.21) | copy-start | bytes 2949124
  410.1 7.6 %copy-start.52 = (bf16[512,12,64]{0,2,1:T(8,128)(2,1)S(1)}, bf16[512,12,64]{0,2,1:T(8,128)(2,1)}, u32[]{:S(2)}) copy-start(bf16[512,12,64]{0,2,1:T(8,128)(2,1)} %copy-done.51) | copy-start | bytes 2359300
  410.1 8.5 %copy-start.97 = (bf16[640,3072]{1,0:T(8,128)(2,1)S(1)}, bf16[640,3072]{1,0:T(8,128)(2,1)}, u32[]{:S(2)}) copy-start(bf16[640,3072]{1,0:T(8,128)(2,1)} %copy-done.96) | copy-start | bytes 11796484
  434.4 128.0 %copy-start.78 = (f32[256]{0:T(256)S(1)}, f32[256]{0:T(256)}, u32[]{:S(2)}) copy-start(f32[256]{0:T(256)} %get-tuple-element.157) | copy-start | bytes 3076
  434.4 128.0 %copy-start.77 = (f32[256]{0:T(256)S(1)}, f32[256]{0:T(256)}, u32[]{:S(2)}) copy-start(f32[256]{0:T(256)} %get-tuple-element.159) | copy-start | bytes 3076
  434.4 128.1 %copy-start.69 = (f32[768]{0:T(1024)S(1)}, f32[768]{0:T(1024)}, u32[]{:S(2)}) copy-start(f32[768]{0:T(1024)} %get-tuple-element.153) | copy-start | bytes 9220
  434.4 128.2 %copy-start.68 = (f32[768]{0:T(1024)S(1)}, f32[768]{0:T(1024)}, u32[]{:S(2)}) copy-start(f32[768]{0:T(1024)} %get-tuple-element.156) | copy-start | bytes 9220
  434.4 128.3 %copy-start.80 = (f32[768]{0:T(1024)S(1)}, f32[768]{0:T(1024)}, u32[]{:S(2)}) copy-start(f32[768]{0:T(1024)} %get-tuple-element.151) | copy-start | bytes 9220
  434.5 128.4 %copy-start.79 = (f32[768]{0:T(1024)S(1)}, f32[768]{0:T(1024)}, u32[]{:S(2)}) copy-start(f32[768]{0:T(1024)} %get-tuple-element.155) | copy-start | bytes 9220
  434.5 148.3 %copy-start.84 = (f32[32]{0:T(128)S(1)}, f32[32]{0:T(128)}, u32[]{:S(2)}) copy-start(f32[32]{0:T(128)} %copy-done.83) | copy-start | bytes 388
  434.5 148.3 %copy-start.90 = (f32[1,160]{1,0:T(1,128)S(1)}, f32[1,160]{1,0:T(1,128)}, u32[]{:S(2)}) copy-start(f32[1,160]{1,0:T(1,128)} %copy-done.89) | copy-start | bytes 1924
  (60 other events, 155.2 us)

commit v2 on v1

--- a/solution.py
+++ b/solution.py
@@ -281,6 +281,445 @@
             place += count
         results.append(outs)
     return results
+
+
+def place_owner(order, place):
+    bits = len(order)
+    return sum(((place >> (bits - 1 - spot)) & 1) * mask for spot, mask in enumerate(order))
+
+
+class Piece:
+    def __init__(self, rows, stages, send, own, land, tail, tail_land, out, send_sem, recv_sem):
+        self.rows, self.stages = rows, stages
+        self.send, self.own, self.land = send, own, land
+        self.tail, self.tail_land, self.out = tail, tail_land, out
+        self.send_sem, self.recv_sem = send_sem, recv_sem
+        self.sizes = [rows * 2 ** (stages - 1 - stage) for stage in range(stages)]
+        self.spots = [sum(self.sizes[:stage]) for stage in range(stages)]
+
+    def copy(self, stage, partner, bit):
+        size = self.sizes[stage]
+        away = pl.multiple_of((1 - bit) * size, 8 if stage == self.stages - 1 else 16)
+        if stage == 0:
+            source, target = self.send.at[:, pl.ds(away, size)], self.land.at[:, pl.ds(0, size)]
+        elif stage < self.stages - 1:
+            spot = pl.multiple_of(self.spots[stage - 1] + away, 16)
+            source = self.land.at[:, pl.ds(spot, size)]
+            target = self.land.at[:, pl.ds(self.spots[stage], size)]
+        else:
+            source, target = self.tail.at[:, pl.ds(away, size)], self.tail_land
+        return pltpu.make_async_remote_copy(
+            src_ref=source,
+            dst_ref=target,
+            send_sem=self.send_sem.at[stage],
+            recv_sem=self.recv_sem.at[stage],
+            device_id=(partner,),
+            device_id_type=MESH_ID,
+        )
+
+    def held(self, stage, bit):
+        size = self.sizes[stage]
+        if stage == 0 and self.own is not None:
+            return self.own, 0
+        if stage == 0:
+            return self.send, pl.multiple_of(bit * size, 16)
+        return self.land, pl.multiple_of(self.spots[stage - 1] + bit * size, 16)
+
+    def add(self, stage, bit, half_index):
+        size = self.sizes[stage]
+        half = size // 2
+        unit = 48 if half % 48 == 0 else 16
+        start = half_index * half
+        source, base = self.held(stage, bit)
+        for slot in range(self.land.shape[0]):
+
+            def step(index, carry, slot=slot):
+                row = pl.multiple_of(start + index * unit, 16)
+                mine = source[slot, pl.ds(pl.multiple_of(base + row, 16), unit)]
+                spot = pl.ds(pl.multiple_of(self.spots[stage] + row, 16), unit)
+                theirs = self.land[slot, spot]
+                total = mine.astype(jnp.float32) + theirs.astype(jnp.float32)
+                self.land[slot, spot] = total.astype(jnp.bfloat16)
+                return carry
+
+            lax.fori_loop(0, half // unit, step, 0)
+
+    def add_tail(self, stage, bit):
+        size = self.sizes[stage]
+        source, base = self.held(stage, bit)
+        for slot in range(self.land.shape[0]):
+            mine = source[slot, pl.ds(base, size)]
+            theirs = self.land[slot, pl.ds(self.spots[stage], size)]
+            self.tail[slot] = mine.astype(jnp.float32) + theirs.astype(jnp.float32)
+
+    def finish(self, bit):
+        size = self.sizes[-1]
+        for slot in range(self.out.shape[0]):
+            mine = self.tail[slot, pl.ds(pl.multiple_of(bit * size, 8), size)]
+            self.out[slot] = mine + self.tail_land[slot]
+
+
+class Stream:
+    def __init__(self, order, partner_of, pieces):
+        self.order, self.partner_of, self.pieces = order, partner_of, pieces
+        self.stages = len(order)
+
+    def launch(self, stage):
+        partner, bit = self.partner_of[self.order[stage]]
+        for piece in self.pieces:
+            piece.copy(stage, partner, bit).start()
+
+    def advance(self, stage):
+        partner, bit = self.partner_of[self.order[stage]]
+        for piece in self.pieces:
+            piece.copy(stage, partner, bit).wait()
+        if stage == self.stages - 1:
+            for piece in self.pieces:
+                piece.finish(bit)
+        elif stage == self.stages - 2:
+            for piece in self.pieces:
+                piece.add_tail(stage, bit)
+            self.launch(stage + 1)
+        else:
+            following = self.partner_of[self.order[stage + 1]][1]
+            for piece in self.pieces:
+                piece.add(stage, bit, 1 - following)
+            self.launch(stage + 1)
+            for piece in self.pieces:
+                piece.add(stage, bit, following)
+
+
+def partners(me, masks):
+    result = {}
+    for mask in masks:
+        bit = lax.rem(lax.div(me, mask), 2)
+        result[mask] = (me + mask - 2 * mask * bit, bit)
+    return result
+
+
+def greet_partners(partner_of):
+    barrier = pltpu.get_barrier_semaphore()
+    for partner, _ in partner_of.values():
+        pl.semaphore_signal(barrier, inc=1, device_id=(partner,), device_id_type=MESH_ID)
+    pl.semaphore_wait(barrier, len(partner_of))
+
+
+EARLY = ((0, 3, 24, 768), (0, 1, 24, 256), (1, 4, 24, 768), (2, 2, 24, 768))
+LATE = ((0, 2, 24, 768), (0, 1, 8, 768), (1, 2, 24, 768), (2, 2, 24, 768))
+
+
+def piece_scratch(spec, stages, source, own):
+    _, slots, rows, width = spec
+    owners = 2**stages
+    shapes = []
+    if source:
+        shapes.append(pltpu.VMEM((slots, rows * owners, width), jnp.bfloat16))
+    if own:
+        shapes.append(pltpu.VMEM((slots, rows * owners // 2, width), jnp.bfloat16))
+    shapes += [
+        pltpu.VMEM((slots, rows * (owners - 2), width), jnp.bfloat16),
+        pltpu.VMEM((slots, 2 * rows, width), jnp.float32),
+        pltpu.VMEM((slots, rows, width), jnp.float32),
+        pltpu.SemaphoreType.DMA((stages,)),
+        pltpu.SemaphoreType.DMA((stages,)),
+    ]
+    return shapes
+
+
+def attention_back_kernel(orders, *refs):
+    stages = len(orders[0])
+    refs = list(refs)
+
+    def take(count):
+        taken = refs[:count]
+        del refs[:count]
+        return taken
+
+    early_send = take(len(EARLY))
+    (hidden, qword, qent, keys, values, cgrad, feat_q, feat_k, lse_delta, first_grad) = take(10)
+    (w_ww, w_we, w_ew, w_ee, w_key, w_value, dense, entity_low) = take(8)
+    early_out = take(len(EARLY))
+    late_out = take(len(LATE))
+    words_out, dent_out = take(2)
+    early_pieces = []
+    own_copies = []
+    me = lax.axis_index("dp")
+    partner_of = partners(me, orders[0])
+    own_sem = refs.pop()
+    word_weights = []
+    dqw, dqe, dkey, dvalue, prob_s, grad_s, flip, hidden_t, hidden_te, entity_t = refs[-10:]
+    del refs[-10:]
+    early = [[], [], []]
+    for index, spec in enumerate(EARLY):
+        own, land, tail, tail_land, send_sem, recv_sem = take(6)
+        early[spec[0]].append(
+            Piece(
+                spec[2], stages, early_send[index], own, land, tail, tail_land,
+                early_out[index], send_sem, recv_sem,
+            )
+        )
+        bit = partner_of[orders[spec[0]][0]][1]
+        size = spec[2] * 2 ** (stages - 1)
+        own_copies.append(
+            pltpu.make_async_copy(
+                early_send[index].at[:, pl.ds(pl.multiple_of(bit * size, 16), size)],
+                own,
+                own_sem.at[index],
+            )
+        )
+    late, late_source = [[], [], []], []
+    for index, spec in enumerate(LATE):
+        source, land, tail, tail_land, send_sem, recv_sem = take(6)
+        late_source.append(source)
+        late[spec[0]].append(
+            Piece(
+                spec[2], stages, source, None, land, tail, tail_land,
+                late_out[index], send_sem, recv_sem,
+            )
+        )
+    spare = early[1][0].own
+    half_rows = w_ww.shape[0] // 2
+    for index, weight in enumerate((w_ww, w_we)):
+        for part in range(2):
+            word_weights.append(
+                pltpu.make_async_copy(
+                    weight.at[pl.ds(part * half_rows, half_rows)],
+                    spare.at[2 * index + part],
+                    own_sem.at[len(EARLY) + 2 * index + part],
+                )
+            )
+    early = [Stream(orders[i], partner_of, early[i]) for i in range(3)]
+    late = [Stream(orders[i], partner_of, late[i]) for i in range(3)]
+
+    greet_partners(partner_of)
+    for stream in early:
+        stream.launch(0)
+    for copy in own_copies:
+        copy.start()
+
+    width = hidden.shape[1]
+    seq_len = hidden.shape[0]
+    words = words_out.shape[0]
+    block = 128
+    lane = lax.broadcasted_iota(jnp.int32, (1, block), 1)
+    low_half = (lane < HD).astype(jnp.float32).astype(jnp.bfloat16)
+    high_half = (lane >= HD).astype(jnp.float32).astype(jnp.bfloat16)
+    halves = (low_half, high_half)
+
+    def flip_step(index, carry):
+        at = pl.ds(pl.multiple_of(index * block, block), block)
+        flip[at] = hidden[:, at].astype(jnp.float32).T
+        return carry
+
+    lax.fori_loop(0, width // block, flip_step, 0)
+    owners = 2**stages
+    rows = width // owners
+    for slot, order in enumerate(orders):
+        begin = words if slot == 2 else 0
+        for pair in range(owners // 2):
+            one, two = place_owner(order, 2 * pair), place_owner(order, 2 * pair + 1)
+            both = jnp.concatenate(
+                [flip[one * rows : one * rows + rows, begin:], flip[two * rows : two * rows + rows, begin:]],
+                axis=0,
+            ).astype(jnp.bfloat16)
+            if slot == 2:
+                hidden_te[pair * 2 * rows : (pair + 1) * 2 * rows] = both
+            else:
+                hidden_t[slot, pair * 2 * rows : (pair + 1) * 2 * rows] = both
+
+    def pair_step(pair, carry):
+        lanes = pl.ds(pl.multiple_of(pair * block, block), block)
+        key_pair = keys[:, lanes]
+        value_pair = values[:, lanes]
+        key_feat = [key_pair * halves[h] + feat_k[...] * halves[1 - h] for h in range(2)]
+        key_only = [key_pair * halves[h] for h in range(2)]
+        value_only = [value_pair * halves[h] for h in range(2)]
+
+        def row_step(index, inner):
+            at = pl.ds(pl.multiple_of(index * block, block), block)
+            qw = qword[at, lanes]
+            qe = qent[at, lanes]
+            feats = feat_q[at]
+            given = cgrad[at, lanes]
+            stats = lse_delta[at]
+            spot = lax.broadcasted_iota(jnp.int32, (1, block), 1) - 4 * pair
+            total_w = jnp.zeros((block, block), jnp.float32)
+            total_e = jnp.zeros((block, block), jnp.float32)
+            for h in range(2):
+                left_w = qw * halves[h] + feats * halves[1 - h]
+                left_e = qe * halves[h] + feats * halves[1 - h]
+                scores = jnp.concatenate(
+                    [
+                        dot_right_t(left_w, key_feat[h][:words]),
+                        dot_right_t(left_e, key_feat[h][words:]),
+                    ],
+                    axis=1,
+                )
+                prob = jnp.exp(scores - jnp.sum(jnp.where(spot == h, stats, 0.0), axis=1, keepdims=True))
+                pgrad = dot_right_t(given, value_only[h])
+                sgrad = (prob * (pgrad - jnp.sum(jnp.where(spot == 2 + h, stats, 0.0), axis=1, keepdims=True))).astype(jnp.bfloat16)
+                prob_s[h, at] = prob.astype(jnp.bfloat16)
+                grad_s[h, at] = sgrad
+                total_w += dot_plain(sgrad[:, :words], key_only[h][:words])
+                total_e += dot_plain(sgrad[:, words:], key_only[h][words:])
+            dqw[at, lanes] = total_w.astype(jnp.bfloat16)
+            dqe[at, lanes] = total_e.astype(jnp.bfloat16)
+            return inner
+
+        lax.fori_loop(0, seq_len // block, row_step, 0)
+        qw_all, qe_all, given_all = qword[:, lanes], qent[:, lanes], cgrad[:, lanes]
+        dkey[:words, lanes] = (
+            dot_left_t(grad_s[0, :, :words], qw_all * halves[0])
+            + dot_left_t(grad_s[1, :, :words], qw_all * halves[1])
+        ).astype(jnp.bfloat16)
+        dkey[words:, lanes] = (
+            dot_left_t(grad_s[0, :, words:], qe_all * halves[0])
+            + dot_left_t(grad_s[1, :, words:], qe_all * halves[1])
+        ).astype(jnp.bfloat16)
+        dvalue[:, lanes] = (
+            dot_left_t(prob_s[0], given_all * halves[0])
+            + dot_left_t(prob_s[1], given_all * halves[1])
+        ).astype(jnp.bfloat16)
+
+        @pl.when(pair == 2)
+        def _():
+            for copy in own_copies:
+                copy.wait()
+            for stream in early:
+                stream.advance(0)
+            for copy in word_weights:
+                copy.start()
+
+        return carry
+
+    lax.fori_loop(0, width // block, pair_step, 0)
+
+    query_scale = HD ** (-0.5)
+    column = 384
+
+    def weight_grad(source, slot, order_slot, grad, begin, end, scale):
+        for cut in range(0, width, column):
+            left = hidden_te[...] if order_slot == 2 else hidden_t[order_slot, :, begin:end]
+            piece = dot_plain(left, grad[begin:end, cut : cut + column])
+            if scale:
+                piece = piece * query_scale
+            source[slot, :, cut : cut + column] = piece.astype(jnp.bfloat16)
+
+    weight_grad(late_source[2], 0, 1, dkey, 0, seq_len, False)
+    weight_grad(late_source[2], 1, 1, dvalue, 0, seq_len, False)
+    late[1].launch(0)
+    for stream in early:
+        stream.advance(1)
+    weight_grad(late_source[3], 0, 2, dqw, words, seq_len, True)
+    weight_grad(late_source[3], 1, 2, dqe, words, seq_len, True)
+    late[2].launch(0)
+
+    def spare_weight(index):
+        return spare[2 * index : 2 * index + 2].reshape(width, width)
+
+    def data_grad(begin, size, word_w, ent_w):
+        at = pl.ds(begin, size)
+        queries = dot_right_t(dqw[at], word_w()) + dot_right_t(dqe[at], ent_w())
+        return (
+            first_grad[at]
+            + query_scale * queries
+            + dot_right_t(dkey[at], w_key[...])
+            + dot_right_t(dvalue[at], w_value[...])
+        )
+
+    state_low = data_grad(words, seq_len - words, lambda: w_ew[...], lambda: w_ee[...]).astype(jnp.bfloat16)
+    dent_out[...] = dot_right_t(state_low, dense[...])
+    entity_width = dense.shape[0]
+    few = entity_width // owners
+    for cut in range(0, entity_width, block):
+        flip[cut : cut + block, :block] = entity_low[:, cut : cut + block].astype(jnp.float32).T
+    for pair in range(owners // 2):
+        one, two = place_owner(orders[0], 2 * pair), place_owner(orders[0], 2 * pair + 1)
+        both = jnp.concatenate(
+            [flip[one * few : one * few + few, :block], flip[two * few : two * few + few, :block]],
+            axis=0,
+        )
+        entity_t[pair * 2 * few : (pair + 1) * 2 * few] = both.astype(jnp.bfloat16)
+    late_source[1][0] = dot_plain(entity_t[...], state_low).astype(jnp.bfloat16)
+    weight_grad(late_source[0], 0, 0, dqw, 0, words, True)
+    weight_grad(late_source[0], 1, 0, dqe, 0, words, True)
+    late[0].launch(0)
+    for stream in early:
+        stream.advance(2)
+
+    for copy in word_weights:
+        copy.wait()
+
+    def word_step(index, carry):
+        begin = pl.multiple_of(index * block, block)
+        words_out[pl.ds(begin, block)] = data_grad(begin, block, lambda: spare_weight(0), lambda: spare_weight(1)).astype(jnp.bfloat16)
+        return carry
+
+    lax.fori_loop(0, words // block, word_step, 0)
+    for turn in ((late[1], 0), (late[2], 0), (late[0], 0)):
+        turn[0].advance(turn[1])
+    for stream in early:
+        stream.advance(3)
+    for stream in late:
+        stream.advance(1)
+    for stream in early:
+        stream.advance(4)
+    for stage in (2, 3, 4):
+        for stream in late:
+            stream.advance(stage)
+
+
+def in_order(grad, order):
+    bits = len(order)
+    owners = 2**bits
+    view = grad.reshape((2,) * bits + (grad.shape[0] // owners, grad.shape[1]))
+    spots = tuple(bits - mask.bit_length() for mask in order)
+    return view.transpose(spots + (bits, bits + 1)).reshape(grad.shape)
+
+
+def attention_back(early_grads, inputs, weights, collective_id):
+    devices = lax.axis_size("dp")
+    orders = stage_masks(devices)
+    stages = len(orders[0])
+    hidden = inputs[0]
+    seq_len, width = hidden.shape
+    slots = weights[-1].shape[0]
+    words = seq_len - slots
+    outs = [
+        jax.ShapeDtypeStruct((count, rows, wide), jnp.float32)
+        for _, count, rows, wide in EARLY + LATE
+    ] + [
+        jax.ShapeDtypeStruct((words, width), jnp.bfloat16),
+        jax.ShapeDtypeStruct((slots, weights[-2].shape[0]), jnp.float32),
+    ]
+    scratch = []
+    for spec in EARLY:
+        scratch += piece_scratch(spec, stages, False, True)
+    for spec in LATE:
+        scratch += piece_scratch(spec, stages, True, False)
+    scratch += [pltpu.VMEM((seq_len, width), jnp.bfloat16)] * 4
+    scratch += [pltpu.VMEM((2, seq_len, seq_len), jnp.bfloat16)] * 2
+    scratch += [
+        pltpu.VMEM((width, seq_len), jnp.float32),
+        pltpu.VMEM((2, width, seq_len), jnp.bfloat16),
+        pltpu.VMEM((width, slots), jnp.bfloat16),
+        pltpu.VMEM((weights[-2].shape[0], slots), jnp.bfloat16),
+        pltpu.SemaphoreType.DMA((len(EARLY) + 4,)),
+    ]
+    vmem = pl.BlockSpec(memory_space=pltpu.VMEM)
+    return pl.pallas_call(
+        functools.partial(attention_back_kernel, orders),
+        out_shape=outs,
+        in_specs=[pl.BlockSpec(memory_space=pltpu.HBM)] * len(EARLY)
+        + [vmem] * len(inputs)
+        + [pl.BlockSpec(memory_space=pltpu.HBM)] * 2
+        + [vmem] * (len(weights) - 2),
+        out_specs=[vmem] * len(outs),
+        scratch_shapes=scratch,
+        compiler_params=pltpu.CompilerParams(
+            collective_id=collective_id, has_side_effects=True, vmem_limit_bytes=62 * 2**20
+        ),
+    )(*early_grads, *inputs, *weights)
 
 
 def body(
@@ -480,74 +919,138 @@
     attn_in = first_grad.astype(jnp.bfloat16)
     out_weight_grad = dot_left_t(context_low, attn_in)
     context_grad = dot_right_t(attn_in, out_weight).astype(jnp.bfloat16).reshape(head_shape)
-    scores_again = attn_scores(query_word_h, query_entity_h, key_rows_h, allowed, word_count)
-    attn_prob = jnp.exp(scores_again - row_lse)
-    prob_low = attn_prob.astype(jnp.bfloat16)
-    prob_grad = jnp.einsum(
-        "qhd,khd->hqk", context_grad, values_h, preferred_element_type=jnp.float32
-    )
-    values_grad = jnp.einsum(
-        "hqk,qhd->khd", prob_low, context_grad, preferred_element_type=jnp.float32
-    )
-    values_grad = values_grad.reshape(seq_len, model_width).astype(jnp.bfloat16)
-    row_delta = jnp.sum(attn_prob * prob_grad, axis=2, keepdims=True)
-    score_grad = (attn_prob * (prob_grad - row_delta)).astype(jnp.bfloat16)
-    qword_grad = jnp.einsum(
-        "hqk,khd->qhd",
-        score_grad[:, :, :word_count],
-        key_rows_h[:word_count],
-        preferred_element_type=jnp.float32,
-    )
-    qword_grad = qword_grad.reshape(seq_len, model_width).astype(jnp.bfloat16)
-    qent_grad = jnp.einsum(
-        "hqk,khd->qhd",
-        score_grad[:, :, word_count:],
-        key_rows_h[word_count:],
-        preferred_element_type=jnp.float32,
-    )
-    qent_grad = qent_grad.reshape(seq_len, model_width).astype(jnp.bfloat16)
-    keys_grad = jnp.concatenate(
-        [
-            jnp.einsum(
-                "hqk,qhd->khd",
-                score_grad[:, :, :word_count],
-                query_word_h,
-                preferred_element_type=jnp.float32,
+    fused = model_width % devices == 0 and (model_width // devices) % 8 == 0 and devices == 32
+    if fused:
+        orders = stage_masks(devices)
+        up_low_grad = up_weight_grad.astype(jnp.bfloat16)
+        up_cuts = [
+            in_order(up_low_grad[:, i * model_width : (i + 1) * model_width], orders[2 * (i // 3)])
+            for i in range(4)
+        ]
+        down_view = down_grad.astype(jnp.bfloat16).reshape(devices, 4, -1, model_width)
+        down_cuts = [
+            in_order(down_view[:, i].reshape(model_width, model_width), orders[1 + i // 3])
+            for i in range(4)
+        ]
+        early_grads = [
+            jnp.stack(up_cuts[:3]),
+            in_order(head_weight_grad.astype(jnp.bfloat16), orders[0])[None],
+            jnp.stack(down_cuts[:3] + [in_order(out_weight_grad.astype(jnp.bfloat16), orders[1])]),
+            jnp.stack([up_cuts[3], down_cuts[3]]),
+        ]
+        codes = jnp.arange(128, dtype=jnp.int32)[None, :] % HD
+        same = segment_row[:, None] == codes
+        feat_q = same.astype(jnp.bfloat16)
+        feat_k = jnp.where(same | (codes >= 4), 0.0, MASKED).astype(jnp.bfloat16)
+        delta = jnp.sum(
+            (context_low.astype(jnp.float32) * context_grad.reshape(seq_len, model_width)).reshape(
+                seq_len, head_count // 2, 2, HD
             ),
-            jnp.einsum(
-                "hqk,qhd->khd",
-                score_grad[:, :, word_count:],
-                query_entity_h,
-                preferred_element_type=jnp.float32,
-            ),
-        ],
-        axis=0,
-    )
-    keys_grad = keys_grad.reshape(seq_len, model_width).astype(jnp.bfloat16)
-    query_ww_grad = query_scale * dot_left_t(word_part, qword_grad[:word_count])
-    query_ew_grad = query_scale * dot_left_t(entity_part, qword_grad[word_count:])
-    query_we_grad = query_scale * dot_left_t(word_part, qent_grad[:word_count])
-    query_ee_grad = query_scale * dot_left_t(entity_part, qent_grad[word_count:])
-    key_weight_grad = dot_left_t(hidden_low, keys_grad)
-    value_weight_grad = dot_left_t(hidden_low, values_grad)
-    word_back = query_scale * (
-        dot_right_t(qword_grad[:word_count], query_ww)
-        + dot_right_t(qent_grad[:word_count], query_we)
-    )
-    entity_back = query_scale * (
-        dot_right_t(qword_grad[word_count:], query_ew)
-        + dot_right_t(qent_grad[word_count:], query_ee)
-    )
-    hidden_grad = (
-        first_grad
-        + jnp.concatenate([word_back, entity_back], axis=0)
-        + dot_right_t(keys_grad, key_weight)
-        + dot_right_t(values_grad, value_weight)
-    )
-    words_grad = hidden_grad[:word_count].astype(jnp.bfloat16)
-    state_low = hidden_grad[word_count:].astype(jnp.bfloat16)
-    dense_grad = dot_left_t(entity_low, state_low)
-    entity_vec_grad = dot_right_t(state_low, entity_dense)
+            axis=3,
+        )
+        lse_pair = row_lse[:, :, 0].T.reshape(seq_len, head_count // 2, 2)
+        lse_delta = jnp.concatenate([lse_pair, delta], axis=2).reshape(seq_len, 2 * head_count)
+        lse_delta = jnp.pad(lse_delta, ((0, 0), (0, 128 - 2 * head_count)))
+        fused_out = attention_back(
+            early_grads,
+            [
+                hidden_low,
+                query_word,
+                query_entity,
+                key_rows,
+                values,
+                context_grad.reshape(seq_len, model_width),
+                feat_q,
+                feat_k,
+                lse_delta,
+                first_grad,
+            ],
+            [
+                query_ww,
+                query_we,
+                query_ew,
+                query_ee,
+                key_weight,
+                value_weight,
+                entity_dense,
+                entity_low,
+            ],
+            7,
+        )
+        up_a, head_a, down_a, mixed, q_word, dense_a, key_value, q_ent, words_grad, entity_vec_grad = (
+            fused_out
+        )
+        up_sum = jnp.concatenate([up_a[0], up_a[1], up_a[2], mixed[0]], axis=1)
+        down_sum = jnp.concatenate([down_a[0], down_a[1], down_a[2], mixed[1]], axis=0)
+    else:
+        scores_again = attn_scores(query_word_h, query_entity_h, key_rows_h, allowed, word_count)
+        attn_prob = jnp.exp(scores_again - row_lse)
+        prob_low = attn_prob.astype(jnp.bfloat16)
+        prob_grad = jnp.einsum(
+            "qhd,khd->hqk", context_grad, values_h, preferred_element_type=jnp.float32
+        )
+        values_grad = jnp.einsum(
+            "hqk,qhd->khd", prob_low, context_grad, preferred_element_type=jnp.float32
+        )
+        values_grad = values_grad.reshape(seq_len, model_width).astype(jnp.bfloat16)
+        row_delta = jnp.sum(attn_prob * prob_grad, axis=2, keepdims=True)
+        score_grad = (attn_prob * (prob_grad - row_delta)).astype(jnp.bfloat16)
+        qword_grad = jnp.einsum(
+            "hqk,khd->qhd",
+            score_grad[:, :, :word_count],
+            key_rows_h[:word_count],
+            preferred_element_type=jnp.float32,
+        )
+        qword_grad = qword_grad.reshape(seq_len, model_width).astype(jnp.bfloat16)
+        qent_grad = jnp.einsum(
+            "hqk,khd->qhd",
+            score_grad[:, :, word_count:],
+            key_rows_h[word_count:],
+            preferred_element_type=jnp.float32,
+        )
+        qent_grad = qent_grad.reshape(seq_len, model_width).astype(jnp.bfloat16)
+        keys_grad = jnp.concatenate(
+            [
+                jnp.einsum(
+                    "hqk,qhd->khd",
+                    score_grad[:, :, :word_count],
+                    query_word_h,
+                    preferred_element_type=jnp.float32,
+                ),
+                jnp.einsum(
+                    "hqk,qhd->khd",
+                    score_grad[:, :, word_count:],
+                    query_entity_h,
+                    preferred_element_type=jnp.float32,
+                ),
+            ],
+            axis=0,
+        )
+        keys_grad = keys_grad.reshape(seq_len, model_width).astype(jnp.bfloat16)
+        query_ww_grad = query_scale * dot_left_t(word_part, qword_grad[:word_count])
+        query_ew_grad = query_scale * dot_left_t(entity_part, qword_grad[word_count:])
+        query_we_grad = query_scale * dot_left_t(word_part, qent_grad[:word_count])
+        query_ee_grad = query_scale * dot_left_t(entity_part, qent_grad[word_count:])
+        key_weight_grad = dot_left_t(hidden_low, keys_grad)
+        value_weight_grad = dot_left_t(hidden_low, values_grad)
+        word_back = query_scale * (
+            dot_right_t(qword_grad[:word_count], query_ww)
+            + dot_right_t(qent_grad[:word_count], query_we)
+        )
+        entity_back = query_scale * (
+            dot_right_t(qword_grad[word_count:], query_ew)
+            + dot_right_t(qent_grad[word_count:], query_ee)
+        )
+        hidden_grad = (
+            first_grad
+            + jnp.concatenate([word_back, entity_back], axis=0)
+            + dot_right_t(keys_grad, key_weight)
+            + dot_right_t(values_grad, value_weight)
+        )
+        words_grad = hidden_grad[:word_count].astype(jnp.bfloat16)
+        state_low = hidden_grad[word_count:].astype(jnp.bfloat16)
+        dense_grad = dot_left_t(entity_low, state_low)
+        entity_vec_grad = dot_right_t(state_low, entity_dense)
     vec_grad = jnp.concatenate([entity_vec_grad, target_grad], axis=0)
     bias_vec_grad = jnp.concatenate(
         [jnp.zeros((slot_count,), jnp.float32), jnp.full((mask_count,), -grad_scale, jnp.float32)]
@@ -591,33 +1094,54 @@
     block = jnp.pad(block, ((0, 0), (0, 128 - spots[-1])))[:, None, :]
     vector_sums = jnp.sum(direct_swap(jnp.pad(block, ((0, 0), (0, 7), (0, 0))), 6)[:, 0], axis=0)
     vector_out = [vector_sums[spots[i] : spots[i + 1]] for i in range(len(cuts))]
-    sums = sum_all(
-        [
-            [up_weight_grad, out_weight_grad, head_weight_grad],
-            [down_grad, query_ww_grad, dense_grad],
-            [query_we_grad, query_ew_grad, query_ee_grad, key_weight_grad, value_weight_grad],
-        ],
-        7,
-    )
-    all_sums = (
-        sums[0][2],
-        vector_out[0],
-        vector_out[1],
-        vector_out[2],
-        vector_out[3],
-        sums[0][0],
-        sums[1][0],
-        vector_out[4],
-        vector_out[5],
-        sums[0][1],
-        sums[1][1],
-        sums[2][0],
-        sums[2][1],
-        sums[2][2],
-        sums[2][3],
-        sums[2][4],
-        sums[1][2],
-    )
+    if fused:
+        all_sums = (
+            head_a[0],
+            vector_out[0],
+            vector_out[1],
+            vector_out[2],
+            vector_out[3],
+            up_sum,
+            down_sum,
+            vector_out[4],
+            vector_out[5],
+            down_a[3],
+            q_word[0],
+            q_word[1],
+            q_ent[0],
+            q_ent[1],
+            key_value[0],
+            key_value[1],
+            dense_a[0],
+        )
+    else:
+        sums = sum_all(
+            [
+                [up_weight_grad, out_weight_grad, head_weight_grad],
+                [down_grad, query_ww_grad, dense_grad],
+                [query_we_grad, query_ew_grad, query_ee_grad, key_weight_grad, value_weight_grad],
+            ],
+            7,
+        )
+        all_sums = (
+            sums[0][2],
+            vector_out[0],
+            vector_out[1],
+            vector_out[2],
+            vector_out[3],
+            sums[0][0],
+            sums[1][0],
+            vector_out[4],
+            vector_out[5],
+            sums[0][1],
+            sums[1][1],
+            sums[2][0],
+            sums[2][1],
+            sums[2][2],
+            sums[2][3],
+            sums[2][4],
+            sums[1][2],
+        )
     return (
         loss_value,
         layer_out.astype(jnp.bfloat16),

time: 596 us -> 544 us (0.913)
  the two profiles are of different devices: /device:TPU:0 before, /device:TPU:11 now
where the time goes in v2:
time: 544 us; the launch traced here: 533 us
  Pallas kernels  251 us (46%)
  matrix products  127 us (23%)
  local copies, waits for them, and re-layouts  91.6 us (17%)
  other arithmetic  55.3 us (10%)
    pallas_call x7, Pallas kernels, direct_swap(): pl.pallas_call(functools.partial(swap_kernel, devices, gather), out_shape...  126 us
    pallas_call x1, Pallas kernels, attention_back(): pl.pallas_call(functools.partial(attention_back_kernel, orders), out_shap...  125 us
    dot_general x15, matrix products, dot_plain(): return jnp.dot(left_side, right_side, preferred_element_type=jnp.float32)  54.1 us
    dot_general x8, matrix products, dot_right_t(): lax.dot_general(left_side, right_side, (((1,), (1,)), ((), ())), preferre...  32.3 us
    unnamed x159, local copies, waits for them, and re-layouts  22.1 us
    dot_general x6, matrix products, dot_left_t(): lax.dot_general(left_side, right_side, (((0,), (0,)), ((), ())), preferre...  20.1 us

profile of v2, /device:TPU:11, one launch (start us, length us, event | category | flops | bytes accessed | tf_op | source)
XLA Modules:
  0.0 533.0 jit_solution(14333223442611305527)
XLA Ops:
  5.5 11.0 %shard_map.425 = s32[32,8,128]{2,1,0:T(8,128)} custom-call(s32[32,8,128]{2,1,0:T(8,128)} %pad.24.source), custom_call_target="tpu_custom_call" | custom-call | tf_op jit(solution)/shard_map/pallas_call | solution.py:114
  18.3 2.5 gather_fusion.1
  22.5 2.0 gather_fusion
  27.2 15.9 %shard_map.426 = bf16[32,16,384]{2,1,0:T(8,128)(2,1)} custom-call(bf16[32,16,384]{2,1,0:T(8,128)(2,1)} %fusion.44.source), custom_call_target="tpu_custom_call" | custom-call | tf_op jit(solution)/shard_map/pallas_call | solution.py:114
  50.1 2.0 fusion.102
  62.3 2.5 convolution_convert_fusion.4.refs_7_
  68.2 2.1 slice.201
  70.3 2.3 copy.72
  72.6 3.5 convolution_convert_fusion.5.refs_8_
  76.1 2.2 copy.69
  78.3 2.3 fusion.38
  82.9 3.0 copy.73
  86.0 2.3 fusion.40
  90.6 3.1 copy.70
  93.6 4.1 fusion.28
  97.7 4.1 fusion.30
  103.5 3.9 copy-done.6
  107.4 3.6 fusion.8
  111.0 9.4 %fusion.27 = bf16[12,64,640]{2,1,0:T(8,128)(2,1)} fusion(bf16[640,12,64]{0,2,1:T(8,128)(2,1)S(1)} %bitcast.215, f32[12,640,128]{1,2,0:T(8,128)S(1)} %copy-done.8, f32[12,640,512]{1,2,0:T(8,128)} %copy-done.6, f32[12,640]{1,0:T(8,128)S(1)} %fusion.8, f32[12,640]{1,0:T(8,128)S(1)} %fusion.9, pred[640,640]{0,1:T(8,128)(4,1)S(1)} %copy-done.31), kind=kOutput, calls=%fused_computation.77 | convolution fusion | flops 654213120 | bytes 22097920 | tf_op jit(solution)/shard_map/hqk,khd->qhd/dot_general | solution.py:820
  121.1 2.9 fusion.100
  125.8 2.3 copy.91
  128.1 23.9 %multiply_convert_fusion.1 = (bf16[640,3072]{1,0:T(8,128)(2,1)S(1)}, f32[640,3072]{1,0:T(8,128)}, f32[640,3072]{1,0:T(8,128)}) fusion(bf16[768,3072]{1,0:T(8,128)(2,1)} %param.48, f32[640,768]{1,0:T(8,128)} %copy-done.13, f32[768]{0:T(1024)S(1)} %copy-done.77, f32[768]{0:T(1024)S(1)} %copy-done.69, f32[640]{0:T(1024)S(1)} %fusion.72, ...), kind=kOutput, calls=%fused_computation.28 | convolution fusion | flops 3150151680 | bytes 26356736 | tf_op jit(solution)/shard_map/dot_general | solution.py:20
  152.0 7.2 %fusion.101 = (f32[640]{0:T(1024)S(1)}, f32[640,768]{1,0:T(8,128)S(1)}) fusion(bf16[640,3072]{1,0:T(8,128)(2,1)S(1)} %get-tuple-element.219, bf16[3072,768]{1,0:T(8,128)(2,1)} %param.49, f32[768]{0:T(1024)S(1)} %copy-done.77, f32[768]{0:T(1024)S(1)} %copy-done.69, f32[640]{0:T(1024)S(1)} %fusion.72, f32[640,768]{1,0:T(8,128)S(1)} %copy-done.14, ...), kind=kOutput, calls=%fused_computation.233 | convolution fusion | flops 3022847488 | bytes 12596736 | tf_op jit(solution)/shard_map/dot_general | solution.py:20
  166.2 18.5 %shard_map.427 = bf16[32,32,256]{2,1,0:T(8,128)(2,1)} custom-call(bf16[32,256]{1,0:T(8,128)(2,1)} %copy-done.47), custom_call_target="tpu_custom_call" | custom-call | tf_op jit(solution)/shard_map/pallas_call | solution.py:114
  184.7 16.7 %while.27 = (s32[]{:T(128)}, f32[2,512]{1,0:T(2,128)}, f32[2,512]{1,0:T(2,128)}, s32[2]{0:T(128)}, bf16[1024,256]{1,0:T(8,128)(2,1)}, /*index=5*/bf16[3968,256]{...) while((s32[]{:T(128)}, f32[2,512]{1,0:T(2,128)}, ...), condition=%wide.region_11.12_spmd, body=%wide.region_8.11_spmd.sunk | while | flops 1050344448 | bytes 18592956 | solution.py:853
  186.6 2.3 add_reduce_fusion.2
  195.0 2.3 add_reduce_fusion.2
  204.1 16.4 %shard_map.428 = f32[32,24,128]{2,1,0:T(8,128)} custom-call(f32[24,128]{1,0:T(8,128)} %maximum_maximum_fusion.source), custom_call_target="tpu_custom_call" | custom-call | tf_op jit(solution)/shard_map/pallas_call | solution.py:114
  227.2 25.3 %while.28 = (s32[]{:T(128)}, f32[3968,256]{1,0:T(8,128)}, f32[3968]{0:T(1024)S(1)}, f32[2,512,256]{2,1,0:T(8,128)}, s32[2]{0:T(128)}, /*index=5*/bf16[1024,256]{...) while((s32[]{:T(128)}, f32[3968,256]{1,0:T(8,128)}, ...), condition=%wide.region_20.21_spmd.clone, body=%wide.region_18.20_spmd.clone.sunk | while | flops 3134787584 | bytes 68505448 | solution.py:889
  229.6 3.2 convert_reduce_fusion.3
  235.1 3.0 convolution_add_fusion.2
  242.1 3.2 convert_reduce_fusion.3
  247.5 3.0 convolution_add_fusion.2
  252.6 29.8 %shard_map.429 = f32[32,32,256]{2,1,0:T(8,128)} custom-call(f32[32,32,256]{2,1,0:T(8,128)} %bitcast.211), custom_call_target="tpu_custom_call" | custom-call | tf_op jit(solution)/shard_map/pallas_call | solution.py:114
  288.7 2.0 multiply_reduce_fusion.1
  292.9 11.2 %add_convert_fusion = bf16[640,3072]{1,0:T(8,128)(2,1)} fusion(f32[640,3072]{1,0:T(8,128)} %get-tuple-element.220, f32[640,3072]{1,0:T(8,128)} %get-tuple-element.262, bf16[3072,768]{1,0:T(8,128)(2,1)} %param.49, f32[640,768]{1,0:T(8,128)S(1)} %get-tuple-element.212, f32[640]{0:T(1024)S(1)} %negate_multiply_fusion.3), kind=kOutput, calls=%fused_computation.27 | convolution fusion | flops 3048407040 | bytes 26348032 | tf_op jit(solution)/shard_map/dot_general | solution.py:30
  305.4 6.7 %convolution_convert_fusion = bf16[3072,768]{1,0:T(8,128)(2,1)S(1)} fusion(bf16[640,3072]{1,0:T(8,128)(2,1)} %copy-done.81, f32[640,768]{1,0:T(8,128)} %copy-done.34, f32[640]{0:T(1024)S(1)} %negate_multiply_fusion.3), kind=kOutput, calls=%fused_computation.42 | convolution fusion | flops 3023241216 | bytes 10619392 | tf_op jit(solution)/shard_map/dot_general | solution.py:24
  316.9 6.2 %multiply_reduce_fusion = (f32[768]{0:T(1024)S(1)}, f32[640]{0:T(1024)S(1)}, f32[768]{0:T(1024)S(1)}, f32[640,768]{1,0:T(8,128)S(1)}) fusion(f32[640,768]{1,0:T(8,128)S(1)} %copy-done.15, f32[640]{0:T(1024)S(1)} %copy-done.63, f32[640]{0:T(1024)S(1)} %broadcast_multiply_fusion.1, f32[768]{0:T(1024)S(1)} %copy-done.70, bf16[640,3072]{1,0:T(8,128)(2,1)S(1)} %copy-done.80, ...), kind=kOutput, calls=%fused_computation.58 | convolution fusion | flops 3024811776 | bytes 14568448 | tf_op jit(solution)/shard_map/dot_general | solution.py:30
  323.8 4.8 convolution_convert_fusion.1
  334.6 12.9 %shard_map.432 = f32[32,8,128]{2,1,0:T(8,128)} custom-call(f32[32,8,128]{2,1,0:T(8,128)} %pad.29.source), custom_call_target="tpu_custom_call" | custom-call | tf_op jit(solution)/shard_map/pallas_call | solution.py:114
  349.7 2.3 convolution_convert_fusion.2
  354.6 2.0 pad_maximum_fusion.1.refs_0_
  358.3 2.4 pad_maximum_fusion.refs_2_
  360.7 2.6 convert_multiply_fusion
  366.4 125.1 %shard_map.430 = (f32[3,24,768]{2,1,0:T(8,128)}, f32[1,24,256]{2,1,0:T(8,128)}, f32[4,24,768]{2,1,0:T(8,128)}, f32[2,24,768]{2,1,0:T(8,128)}, f32[2,24,768]{2,1,...) custom-call(bf16[3,768,768]{2,1,0:T(8,128)(2,1)} %pad_maximum_fusion, ...), custom_call_target="tpu_custom_call" | custom-call | tf_op jit(solution)/shard_map/pallas_call | solution.py:710
  493.8 21.0 %shard_map.431 = bf16[32,16,384]{2,1,0:T(8,128)(2,1)} custom-call(bf16[32,16,384]{2,1,0:T(8,128)(2,1)} %fusion.45.source), custom_call_target="tpu_custom_call" | custom-call | tf_op jit(solution)/shard_map/pallas_call | solution.py:114
  515.9 3.3 scatter_fusion.1
  519.4 6.3 %scatter_fusion = f32[3968,256]{1,0:T(8,128)} fusion(f32[3968,256]{1,0:T(8,128)} %get-tuple-element.124, s32[320]{0:T(512)S(1)} %copy-done.58, f32[320,256]{1,0:T(8,128)S(1)} %reshape.420), kind=kCustom, calls=%fused_computation.2 | custom fusion | flops 81920 | bytes 984320 | tf_op jit(solution)/shard_map/scatter-add | solution.py:1075
  (329 shorter events, 116.3 us)
Async XLA Ops:
  0.7 120.4 %copy-start = (bf16[768,768]{1,0:T(8,128)(2,1)S(1)}, bf16[768,768]{1,0:T(8,128)(2,1)}, u32[]{:S(2)}) copy-start(bf16[768,768]{1,0:T(8,128)(2,1)} %param.45) | copy-start | bytes 3538948
  0.7 17.6 %copy-start.1 = (bf16[3968]{0:T(1024)(128)(2,1)S(1)}, bf16[3968]{0:T(1024)(128)(2,1)}, u32[]{:S(2)}) copy-start(bf16[3968]{0:T(1024)(128)(2,1)} %param.37) | copy-start | bytes 23812
  3.3 43.3 %copy-start.59 = (s32[320]{0:T(512)}, s32[320]{0:T(512)S(1)}, u32[]{:S(2)}) copy-start(s32[320]{0:T(512)S(1)} %eq.74) | copy-start | bytes 3844
  18.3 4.2 copy-start.7
  78.3 3.5 copy-start.33
  86.0 3.5 copy-start.32
  97.7 4.1 copy-start.8
  97.7 4.1 copy-start.31
  101.9 5.5 %copy-start.6 = (f32[12,640,512]{1,2,0:T(8,128)}, f32[12,640,512]{1,2,0:T(8,128)S(1)}, u32[]{:S(2)}) copy-start(f32[12,640,512]{1,2,0:T(8,128)S(1)} %fusion.30) | copy-start | bytes 47185924
  107.4 3.6 copy-start.40
  124.0 4.0 copy-start.69
  124.0 4.0 copy-start.77
  125.7 26.3 %copy-start.54 = (f32[640]{0:T(1024)}, f32[640]{0:T(1024)S(1)}, u32[]{:S(2)}) copy-start(f32[640]{0:T(1024)S(1)} %multiply_reduce_fusion.5) | copy-start | bytes 7684
  125.7 26.2 %copy-start.62 = (f32[640]{0:T(1024)}, f32[640]{0:T(1024)S(1)}, u32[]{:S(2)}) copy-start(f32[640]{0:T(1024)S(1)} %fusion.72) | copy-start | bytes 7684
  128.0 24.0 %copy-start.14 = (f32[640,768]{1,0:T(8,128)S(1)}, f32[640,768]{1,0:T(8,128)}, u32[]{:S(2)}) copy-start(f32[640,768]{1,0:T(8,128)} %copy-done.13) | copy-start | bytes 5898244
  152.0 7.2 %copy-start.81 = (bf16[640,3072]{1,0:T(8,128)(2,1)}, bf16[640,3072]{1,0:T(8,128)(2,1)S(1)}, u32[]{:S(2)}) copy-start(bf16[640,3072]{1,0:T(8,128)(2,1)S(1)} %get-tuple-element.219) | copy-start | bytes 11796484
  152.0 7.6 %copy-start.53 = (f32[768]{0:T(1024)S(1)}, f32[768]{0:T(1024)}, u32[]{:S(2)}) copy-start(f32[768]{0:T(1024)} %param.50) | copy-start | bytes 9220
  152.0 7.6 %copy-start.68 = (f32[768]{0:T(1024)S(1)}, f32[768]{0:T(1024)}, u32[]{:S(2)}) copy-start(f32[768]{0:T(1024)} %param.51) | copy-start | bytes 9220
  159.6 3.4 copy-start.61
  159.7 3.4 copy-start.73
  159.7 4.7 copy-start.76
  162.3 22.4 %copy-start.64 = (f32[32]{0:T(128)}, f32[32]{0:T(128)S(1)}, u32[]{:S(2)}) copy-start(f32[32]{0:T(128)S(1)} %broadcast_multiply_fusion.2) | copy-start | bytes 388
  163.0 21.7 %copy-start.66 = (f32[32]{0:T(128)}, f32[32]{0:T(128)S(1)}, u32[]{:S(2)}) copy-start(f32[32]{0:T(128)S(1)} %fusion.76) | copy-start | bytes 388
  184.7 42.5 %copy-start.2 = (f32[3968]{0:T(1024)S(1)}, f32[3968]{0:T(1024)}, u32[]{:S(2)}) copy-start(f32[3968]{0:T(1024)} %custom-call.1) | copy-start | bytes 47620
  229.6 3.2 copy-start.38
  242.1 3.2 copy-start.38
  252.5 31.1 %copy-start.65 = (f32[32]{0:T(128)S(1)}, f32[32]{0:T(128)}, u32[]{:S(2)}) copy-start(f32[32]{0:T(128)} %copy-done.64) | copy-start | bytes 388
  252.5 31.8 %copy-start.75 = (f32[32]{0:T(128)S(1)}, f32[32]{0:T(128)}, u32[]{:S(2)}) copy-start(f32[32]{0:T(128)} %copy-done.74) | copy-start | bytes 388
  252.6 31.8 %copy-start.67 = (f32[32]{0:T(128)S(1)}, f32[32]{0:T(128)}, u32[]{:S(2)}) copy-start(f32[32]{0:T(128)} %copy-done.66) | copy-start | bytes 388
  252.6 36.2 %copy-start.10 = (f32[640,768]{1,0:T(8,128)S(1)}, f32[640,768]{1,0:T(8,128)}, u32[]{:S(2)}) copy-start(f32[640,768]{1,0:T(8,128)} %copy-done.9) | copy-start | bytes 5898244
  287.5 3.3 copy-start.30
  316.9 6.2 %copy-start.55 = (f32[640]{0:T(1024)S(1)}, f32[640]{0:T(1024)}, u32[]{:S(2)}) copy-start(f32[640]{0:T(1024)} %copy-done.54) | copy-start | bytes 7684
  328.9 31.8 %copy-start.12 = (f32[640,768]{1,0:T(8,128)}, f32[640,768]{1,0:T(8,128)S(1)}, u32[]{:S(2)}) copy-start(f32[640,768]{1,0:T(8,128)S(1)} %broadcast_add_fusion.refs_13_) | copy-start | bytes 5898244
  366.4 125.1 %copy-start.51 = (f32[32,256]{1,0:T(8,128)S(1)}, f32[32,256]{1,0:T(8,128)}, u32[]{:S(2)}) copy-start(f32[32,256]{1,0:T(8,128)} %get-tuple-element.207) | copy-start | bytes 98308
  366.4 125.1 %copy-start.60 = (s32[320]{0:T(512)S(1)}, s32[320]{0:T(512)}, u32[]{:S(2)}) copy-start(s32[320]{0:T(512)} %copy-done.59) | copy-start | bytes 3844
  366.4 126.6 %copy-start.42 = (bf16[32,10,128]{2,1,0:T(8,128)(2,1)S(1)}, bf16[32,10,128]{2,1,0:T(8,128)(2,1)}, u32[]{:S(2)}) copy-start(bf16[32,10,128]{2,1,0:T(8,128)(2,1)} %broadcast_in_dim.141) | copy-start | bytes 245764
  491.5 24.5 %copy-start.58 = (s32[320]{0:T(512)S(1)}, s32[320]{0:T(512)}, u32[]{:S(2)}) copy-start(s32[320]{0:T(512)} %reshape.418) | copy-start | bytes 3844
  515.9 3.3 copy-start.36
  519.2 6.5 %copy-start.3 = (f32[3968]{0:T(1024)}, f32[3968]{0:T(1024)S(1)}, u32[]{:S(2)}) copy-start(f32[3968]{0:T(1024)S(1)} %scatter_fusion.1) | copy-start | bytes 47620
  519.4 6.4 %copy-start.49 = (f32[2,24,768]{2,1,0:T(8,128)S(1)}, f32[2,24,768]{2,1,0:T(8,128)}, u32[]{:S(2)}) copy-start(f32[2,24,768]{2,1,0:T(8,128)} %get-tuple-element.128) | copy-start | bytes 442372
  519.4 6.3 %copy-start.50 = (f32[2,24,768]{2,1,0:T(8,128)S(1)}, f32[2,24,768]{2,1,0:T(8,128)}, u32[]{:S(2)}) copy-start(f32[2,24,768]{2,1,0:T(8,128)} %get-tuple-element.129) | copy-start | bytes 442372
  519.4 7.1 %copy-start.45 = (f32[3,24,768]{2,1,0:T(8,128)S(1)}, f32[3,24,768]{2,1,0:T(8,128)}, u32[]{:S(2)}) copy-start(f32[3,24,768]{2,1,0:T(8,128)} %get-tuple-element.132) | copy-start | bytes 663556
  519.4 7.0 %copy-start.48 = (f32[2,24,768]{2,1,0:T(8,128)S(1)}, f32[2,24,768]{2,1,0:T(8,128)}, u32[]{:S(2)}) copy-start(f32[2,24,768]{2,1,0:T(8,128)} %get-tuple-element.130) | copy-start | bytes 442372
  519.4 7.7 %copy-start.44 = (f32[4,24,768]{2,1,0:T(8,128)S(1)}, f32[4,24,768]{2,1,0:T(8,128)}, u32[]{:S(2)}) copy-start(f32[4,24,768]{2,1,0:T(8,128)} %get-tuple-element.131) | copy-start | bytes 884740
  519.4 7.7 %copy-start.46 = (f32[2,24,768]{2,1,0:T(8,128)S(1)}, f32[2,24,768]{2,1,0:T(8,128)}, u32[]{:S(2)}) copy-start(f32[2,24,768]{2,1,0:T(8,128)} %get-tuple-element.133) | copy-start | bytes 442372
  525.7 3.6 copy-start.41
  526.5 3.7 copy-start.57
  527.1 3.6 copy-start.56
  (39 other events, 75.4 us)
